TPU v7x, 128 devices: a whole 4x4x4 slice. The times are simulated.
128 devices in a mesh: dp: 4 (over y_hi, core), seq: 32 (over x, y_lo, z).
Axes of the slice: x: 4, y: 4 (y_hi: 2, y_lo: 2; y = y_hi * 2 + y_lo), z: 4, core: 2. Of those that a mesh axis runs over, the one named last changes fastest.
Arguments:
- query_in: bfloat16 [4, 4096, 2048], P('dp', 'seq'), may hold values from -6 to 6
- key_in: bfloat16 [4, 4096, 2048], P('dp', 'seq'), may hold values from -6 to 6
- value_in: bfloat16 [4, 4096, 2048], P('dp', 'seq'), may hold values from -6 to 6
- grad_out: bfloat16 [4, 4096, 2048], P('dp', 'seq'), may hold values from -6 to 6
- filter_taps: float32 [2048, 4096], P('seq'), may hold values from -2 to 2
Outputs:
- grad_query: bfloat16 [4, 4096, 2048], P('dp', 'seq')
- grad_key: bfloat16 [4, 4096, 2048], P('dp', 'seq')
- grad_value: bfloat16 [4, 4096, 2048], P('dp', 'seq')
- grad_filter: float32 [2048, 4096], P('seq', 'dp')
All inputs are finite; a program needn't handle non-finite values.
Results may differ from a plain program's by a relative error of at most 0.013.
Values may be sent and summed in bfloat16 or wider, within the bound.
No kernel may reach another device: no remote copies, remote signals or barrier semaphores. Data moves between devices by JAX's collectives and lax.ppermute only.
A program may use at most 64 MiB of HBM per device.

v0:
```python
import functools

import jax
import jax.numpy as jnp
import ml_dtypes
import numpy as np
from jax import lax
from jax.experimental import pallas as pl
from jax.experimental.pallas import tpu as pltpu
from jax.sharding import PartitionSpec as P

TOKENS = 4096
ROWS = 32
COLS = 128
LANES = 128
HALF = 64
SUB = 8
GROUPS = COLS // SUB
F32 = jnp.float32
BF16 = jnp.bfloat16
VMEM_LIMIT = 48 * 1024 * 1024


@functools.cache
def tables():
    index = np.arange(ROWS)
    token = COLS * index[:, None] + np.arange(COLS)[None, :]
    angle = 2.0 * np.pi * (index[:, None, None] + 0.25) * token[None] / TOKENS
    parts = np.stack([np.cos(angle), -np.sin(angle)])
    parts = parts.reshape(2, ROWS, ROWS, GROUPS, SUB)
    eye = np.eye(SUB)
    first = np.einsum("akpgr,rs->gakrps", parts, eye).reshape(GROUPS, 2 * ROWS * SUB, ROWS * SUB)
    last = np.swapaxes(first, 1, 2) / TOKENS
    turn = 2.0 * np.pi * (np.arange(COLS)[:, None] * np.arange(COLS)[None, :] % COLS) / COLS
    cos, sin = np.cos(turn), np.sin(turn)
    ahead = np.block([[cos, sin], [-sin, cos]])
    back = np.block([[cos, -sin], [sin, cos]])
    kind = ml_dtypes.bfloat16
    return tuple(table.astype(kind) for table in (first, last, ahead, back))


def dot(left, right):
    return jnp.dot(left, right, preferred_element_type=F32)


def lane_low(shape):
    return lax.broadcasted_iota(jnp.int32, shape, len(shape) - 1) < HALF


def swap_halves(block):
    return pltpu.roll(block, HALF, block.ndim - 1)


def split_rows(block, count):
    wide = block.astype(F32)
    low = wide[:, :SUB].reshape(count * SUB, LANES).astype(BF16)
    high = wide[:, SUB:].reshape(count * SUB, LANES).astype(BF16)
    return low, high


def join_rows(low, high, count):
    shape = (count, SUB, LANES)
    return jnp.concatenate([low.reshape(shape), high.reshape(shape)], axis=1)


def first_step(source, first_ref, spread_ref):
    @pl.loop(0, GROUPS // 2)
    def _(step):
        rows = pl.ds(pl.multiple_of(step * 2 * SUB, 2 * SUB), 2 * SUB)
        low, high = split_rows(source[:, rows, :], ROWS)
        joined = join_rows(dot(first_ref[2 * step], low), dot(first_ref[2 * step + 1], high), 2 * ROWS)
        spread_ref[:, rows, :] = joined.astype(BF16)


def last_step(spread_ref, last_ref, store):
    @pl.loop(0, GROUPS // 2)
    def _(step):
        rows = pl.ds(pl.multiple_of(step * 2 * SUB, 2 * SUB), 2 * SUB)
        low, high = split_rows(spread_ref[:, rows, :], 2 * ROWS)
        store(rows, join_rows(dot(last_ref[2 * step], low), dot(last_ref[2 * step + 1], high), ROWS))


def pair_of(spread_ref, step):
    sides = []
    for k in (2 * step, 2 * step + 1):
        sides.append(jnp.concatenate([spread_ref[k], spread_ref[ROWS + k]], axis=0))
    return jnp.concatenate(sides, axis=1)


def gate_kernel(query_ref, key_ref, value_ref, cotan_ref, out_ref):
    low = lane_low((COLS, LANES))
    for block in range(out_ref.shape[0] // 2):
        lanes = pl.ds(block * LANES, LANES)
        gated = key_ref[:, lanes].astype(F32) * value_ref[:, lanes].astype(F32)
        grad = query_ref[:, lanes].astype(F32) * cotan_ref[:, lanes].astype(F32)
        out_ref[2 * block] = jnp.where(low, gated, swap_halves(grad)).astype(BF16)
        out_ref[2 * block + 1] = jnp.where(low, swap_halves(gated), grad).astype(BF16)


def filter_kernel(taps_ref, first_ref, ahead_ref, real_ref, imag_ref, rows_ref, spread_ref):
    for p in range(ROWS):
        block = taps_ref[:, p * COLS : (p + 1) * COLS]
        rows_ref[p] = jnp.concatenate([block, block], axis=0).T.astype(BF16)
    first_step(rows_ref, first_ref, spread_ref)
    low = lane_low((COLS, LANES))

    @pl.loop(0, ROWS // 2)
    def _(step):
        spec = dot(ahead_ref[...], pair_of(spread_ref, step))
        for side in range(2):
            part = spec[:, side * LANES : (side + 1) * LANES]
            real_ref[2 * step + side] = part[:COLS]
            imag_ref[2 * step + side] = jnp.where(low, part[COLS:], -part[COLS:])


def conv_kernel(data_ref, filt_re, filt_im, first_ref, last_ref, ahead_ref, back_ref, out_ref, spec_ref, spread_ref):
    first_step(data_ref, first_ref, spread_ref)

    @pl.loop(0, ROWS // 2)
    def _(step):
        spec = dot(ahead_ref[...], pair_of(spread_ref, step))
        sides = []
        for side in range(2):
            k = 2 * step + side
            real = spec[:COLS, side * LANES : (side + 1) * LANES]
            imag = spec[COLS:, side * LANES : (side + 1) * LANES]
            spec_ref[k] = real
            spec_ref[ROWS + k] = imag
            turn_re, turn_im = filt_re[k], filt_im[k]
            prod_re = turn_re * real - turn_im * imag
            prod_im = turn_re * imag + turn_im * real
            sides.append(jnp.concatenate([prod_re, prod_im], axis=0).astype(BF16))
        result = dot(back_ref[...], jnp.concatenate(sides, axis=1)).astype(BF16)
        for side in range(2):
            k = 2 * step + side
            spread_ref[k] = result[:COLS, side * LANES : (side + 1) * LANES]
            spread_ref[ROWS + k] = result[COLS:, side * LANES : (side + 1) * LANES]

    def store(rows, block):
        out_ref[:, rows, :] = block.astype(BF16)

    last_step(spread_ref, last_ref, store)


def taps_kernel(place_ref, spec_ref, last_ref, back_ref, out_ref, spread_ref, lags_ref):
    @pl.loop(0, ROWS // 2)
    def _(step):
        sides = []
        for side in range(2):
            k = 2 * step + side
            real, imag = spec_ref[k], spec_ref[ROWS + k]
            other_re, other_im = swap_halves(real), swap_halves(imag)
            prod_re = other_re * real + other_im * imag
            prod_im = other_im * real - other_re * imag
            sides.append(jnp.concatenate([prod_re, prod_im], axis=0).astype(BF16))
        result = dot(back_ref[...], jnp.concatenate(sides, axis=1)).astype(BF16)
        for side in range(2):
            k = 2 * step + side
            spread_ref[k] = result[:COLS, side * LANES : (side + 1) * LANES]
            spread_ref[ROWS + k] = result[COLS:, side * LANES : (side + 1) * LANES]

    def store(rows, block):
        lags_ref[:, rows, :] = block

    last_step(spread_ref, last_ref, store)
    place = place_ref[0]
    per = ROWS // 4
    for quarter in range(4):
        slot = jnp.bitwise_xor(place, quarter)
        for p in range(per):
            out_ref[slot, :, p * COLS : (p + 1) * COLS] = lags_ref[quarter * per + p].T[:HALF].astype(BF16)


def mix_kernel(data_ref, key_ref, value_ref, cotan_ref, query_out, key_out, value_out):
    low = lane_low((COLS, LANES))
    for block in range(data_ref.shape[0] // 2):
        lanes = pl.ds(block * LANES, LANES)
        even = data_ref[2 * block].astype(F32)
        odd = data_ref[2 * block + 1].astype(F32)
        conv = jnp.where(low, even, swap_halves(odd))
        grad = jnp.where(low, swap_halves(even), odd)
        query_out[:, lanes] = (cotan_ref[:, lanes].astype(F32) * conv).astype(BF16)
        key_out[:, lanes] = (grad * value_ref[:, lanes].astype(F32)).astype(BF16)
        value_out[:, lanes] = (grad * key_ref[:, lanes].astype(F32)).astype(BF16)


def call(kernel, out_shape, scratch=(), flops=0, nbytes=0, smem=0):
    inside = pl.BlockSpec(memory_space=pltpu.VMEM)
    scalar = pl.BlockSpec(memory_space=pltpu.SMEM)

    def run(*args):
        return pl.pallas_call(
            kernel,
            out_shape=out_shape,
            in_specs=[scalar] * smem + [inside] * (len(args) - smem),
            out_specs=jax.tree.map(lambda _: inside, out_shape),
            scratch_shapes=list(scratch),
            compiler_params=pltpu.CompilerParams(vmem_limit_bytes=VMEM_LIMIT),
            cost_estimate=pl.CostEstimate(flops=flops, bytes_accessed=nbytes, transcendentals=0),
        )(*args)

    return run


def on_device(query_in, key_in, value_in, grad_out, filter_taps):
    first, last, ahead, back = (jnp.asarray(table) for table in tables())
    query, keys, values, cotan = query_in[0], key_in[0], value_in[0], grad_out[0]
    shape = jax.ShapeDtypeStruct
    cube = (ROWS, COLS, LANES)
    unit = 2 * 16 * 512 * 256 * 128
    spread = pltpu.VMEM((2 * ROWS, COLS, LANES), BF16)

    sent = call(gate_kernel, shape(cube, BF16), flops=1 << 21, nbytes=3 << 20)(query, keys, values, cotan)
    filt_re, filt_im = call(
        filter_kernel,
        (shape(cube, F32), shape(cube, F32)),
        [pltpu.VMEM(cube, BF16), spread],
        flops=2 * unit,
        nbytes=10 << 20,
    )(filter_taps, first, ahead)
    data = lax.all_to_all(sent, "seq", split_axis=0, concat_axis=0, tiled=True)
    result, spec = call(
        conv_kernel,
        (shape(cube, BF16), shape((2 * ROWS, COLS, LANES), F32)),
        [spread],
        flops=4 * unit,
        nbytes=18 << 20,
    )(data, filt_re, filt_im, first, last, ahead, back)
    returned = lax.all_to_all(result, "seq", split_axis=0, concat_axis=0, tiled=True)
    place = lax.axis_index("dp").astype(jnp.int32).reshape(1)
    terms = call(
        taps_kernel,
        shape((4, HALF, TOKENS // 4), BF16),
        [spread, pltpu.VMEM(cube, F32)],
        flops=2 * unit,
        nbytes=9 << 20,
        smem=1,
    )(place, spec, last, back)
    total = terms[0].astype(F32)
    for shift in range(1, 4):
        pairs = [(d, d ^ shift) for d in range(4)]
        total = total + lax.ppermute(terms[shift], "dp", pairs).astype(F32)
    grad_filter = total * lax.rsqrt(F32(4 * TOKENS))
    wide = shape(query.shape, BF16)
    grad_query, grad_key, grad_value = call(
        mix_kernel, (wide, wide, wide), flops=1 << 21, nbytes=4 << 20
    )(returned, keys, values, cotan)
    return (grad_query[None], grad_key[None], grad_value[None], grad_filter)


def solution(mesh):
    tokens = P("dp", "seq", None)
    return jax.shard_map(
        on_device,
        mesh=mesh,
        in_specs=(tokens, tokens, tokens, tokens, P("seq", None)),
        out_specs=(tokens, tokens, tokens, P("seq", "dp")),
        check_vma=False,
    )
```

profile of v0, /device:TPU:1, one launch (start us, length us, event | category | flops | bytes accessed | tf_op | source)
XLA Modules:
  0.0 81.3 jit_solution(3513026771810102500)
XLA Ops:
  0.6 0.0 copy-start.1
  0.6 1.0 %copy-done.1 = bf16[1,128,2048]{2,1,0:T(8,128)(2,1)S(1)} copy-done((bf16[1,128,2048]{2,1,0:T(8,128)(2,1)S(1)}, bf16[1,128,2048]{2,1,0:T(8,128)(2,1)}, u32[]{:S(2)}) %copy-start.1) | copy-done | bytes 524312
  1.7 1.0 %copy-done.3 = bf16[1,128,2048]{2,1,0:T(8,128)(2,1)S(1)} copy-done((bf16[1,128,2048]{2,1,0:T(8,128)(2,1)S(1)}, bf16[1,128,2048]{2,1,0:T(8,128)(2,1)}, u32[]{:S(2)}) %copy-start.3) | copy-done | bytes 524312
  2.7 1.0 %copy-done.5 = bf16[1,128,2048]{2,1,0:T(8,128)(2,1)S(1)} copy-done((bf16[1,128,2048]{2,1,0:T(8,128)(2,1)S(1)}, bf16[1,128,2048]{2,1,0:T(8,128)(2,1)}, u32[]{:S(2)}) %copy-start.5) | copy-done | bytes 524312
  3.8 1.0 %copy-done.12 = bf16[1,128,2048]{2,1,0:T(8,128)(2,1)S(1)} copy-done((bf16[1,128,2048]{2,1,0:T(8,128)(2,1)S(1)}, bf16[1,128,2048]{2,1,0:T(8,128)(2,1)}, u32[]{:S(2)}) %copy-start.12) | copy-done | bytes 524312
  4.8 1.5 %shard_map.120 = bf16[32,128,128]{2,1,0:T(8,128)(2,1)} custom-call(bf16[128,2048]{1,0:T(8,128)(2,1)S(1)} %bitcast.25, bf16[128,2048]{1,0:T(8,128)(2,1)S(1)} %bitcast.19, bf16[128,2048]{1,0:T(8,128)(2,1)S(1)} %bitcast.21, bf16[128,2048]{1,0:T(8,128)(2,1)S(1)} %bitcast.23), custom_call_target="tpu_custom_call" | custom-call | flops 2097152 | bytes 3145728 | tf_op jit(solution)/shard_map/pallas_call | solution.py:192
  6.3 9.9 %all-to-all-start = ((bf16[32,128,128]{2,1,0:T(8,128)(2,1)}), bf16[32,128,128]{2,1,0:T(8,128)(2,1)S(1)}, u32[]{:S(2)}, u32[]{:S(2)}) async-start(bf16[32,128,128]{2,1,0:T(8,128)(2,1)} %shard_map.120), calls=%async_computation | async-start | bytes 2097152 | tf_op jit(solution)/shard_map/all_to_all | solution.py:221
  16.2 0.0 copy-done.11
  16.2 0.0 copy-start.9
  16.2 1.2 %copy-done.9 = f32[64,4096]{1,0:T(8,128)S(1)} copy-done((f32[64,4096]{1,0:T(8,128)S(1)}, f32[64,4096]{1,0:T(8,128)}, u32[]{:S(2)}) %copy-start.9) | copy-done | bytes 1048600
  17.4 8.0 %shard_map.121 = (f32[32,128,128]{2,1,0:T(8,128)S(1)}, f32[32,128,128]{2,1,0:T(8,128)S(1)}) custom-call(f32[64,4096]{1,0:T(8,128)S(1)} %copy-done.9, bf16[16,512,256]{2,1,0:T(8,128)(2,1)} %constant.16.clone.first_ref, bf16[256,256]{1,0:T(8,128)(2,1)S(1)} %copy-done.11), custom_call_target="tpu_custom_call" | custom-call | flops 1073741824 | bytes 10485760 | tf_op jit(solution)/shard_map/pallas_call | solution.py:192
  25.5 0.0 copy-start.7
  25.5 1.3 %copy-done.7 = f32[32,128,128]{2,1,0:T(8,128)} copy-done((f32[32,128,128]{2,1,0:T(8,128)}, f32[32,128,128]{2,1,0:T(8,128)S(1)}, u32[]{:S(2)}) %copy-start.7) | copy-done | bytes 2097176
  26.8 4.1 %all-to-all-done.data_ref = bf16[32,128,128]{2,1,0:T(8,128)(2,1)S(1)} async-done(((bf16[32,128,128]{2,1,0:T(8,128)(2,1)}), bf16[32,128,128]{2,1,0:T(8,128)(2,1)S(1)}, u32[]{:S(2)}, u32[]{:S(2)}) %all-to-all-start) | async-done | bytes 1048608 | tf_op jit(solution)/shard_map/all_to_all | solution.py:221
  30.9 0.0 copy-done.10
  30.9 17.4 %shard_map.122 = (bf16[32,128,128]{2,1,0:T(8,128)(2,1)S(1)}, f32[64,128,128]{2,1,0:T(8,128)}) custom-call(bf16[32,128,128]{2,1,0:T(8,128)(2,1)S(1)} %all-to-all-done.data_ref, f32[32,128,128]{2,1,0:T(8,128)S(1)} %get-tuple-element.11.filt_re, f32[32,128,128]{2,1,0:T(8,128)} %copy-done.7, bf16[16,512,256]{2,1,0:T(8,128)(2,1)} %constant.16.clone.first_ref, ...), custom_call_target="tpu_custom_call" | custom-call | flops 2147483648 | bytes 18874368 | tf_op jit(solution)/shard_map/pallas_call | solution.py:192
  48.3 1.0 %copy-done.8 = bf16[32,128,128]{2,1,0:T(8,128)(2,1)} copy-done((bf16[32,128,128]{2,1,0:T(8,128)(2,1)}, bf16[32,128,128]{2,1,0:T(8,128)(2,1)S(1)}, u32[]{:S(2)}) %copy-start.8) | copy-done | bytes 1048600
  49.3 6.0 %all-to-all-start.1 = ((bf16[32,128,128]{2,1,0:T(8,128)(2,1)}), bf16[32,128,128]{2,1,0:T(8,128)(2,1)S(1)}, u32[]{:S(2)}, u32[]{:S(2)}) async-start(bf16[32,128,128]{2,1,0:T(8,128)(2,1)} %copy-done.8), calls=%async_computation.1 | async-start | bytes 2097152 | tf_op jit(solution)/shard_map/all_to_all | solution.py:229
  55.3 0.0 copy-start
  55.3 2.2 %copy-done = f32[64,128,128]{2,1,0:T(8,128)S(1)} copy-done((f32[64,128,128]{2,1,0:T(8,128)S(1)}, f32[64,128,128]{2,1,0:T(8,128)}, u32[]{:S(2)}) %copy-start) | copy-done | bytes 4194328
  57.5 10.1 %shard_map.124 = bf16[4,64,1024]{2,1,0:T(8,128)(2,1)S(1)} custom-call(s32[1]{0:T(128)} %bitcast.7.place_ref, f32[64,128,128]{2,1,0:T(8,128)S(1)} %copy-done, bf16[16,256,512]{2,1,0:T(8,128)(2,1)} %constant.17.clone.last_ref, bf16[256,256]{1,0:T(8,128)(2,1)S(1)} %copy-done.10), custom_call_target="tpu_custom_call" | custom-call | flops 1073741824 | bytes 9437184 | tf_op jit(solution)/shard_map/pallas_call | solution.py:192
  67.6 1.5 %collective-permute-start = (bf16[64,1024]{1,0:T(8,128)(2,1)S(1)}, bf16[64,1024]{1,0:T(8,128)(2,1)S(1)}, u32[]{:S(2)}, u32[]{:S(2)}) collective-permute-start(bf16[64,1024]{1,0:T(8,128)(2,1)S(1)} %get-tuple-element.18), channel_id=1, source_target_pairs={{0,32},{32,0},{64,96},{96,64},{1,33},{33,1},{65,97},{97,65},{2,34}... | collective-permute-start | bytes 393224 | tf_op jit(solution)/shard_map/ppermute | solution.py:242
  69.1 2.6 %collective-permute-start.1 = (bf16[64,1024]{1,0:T(8,128)(2,1)S(1)}, bf16[64,1024]{1,0:T(8,128)(2,1)S(1)}, u32[]{:S(2)}, u32[]{:S(2)}) collective-permute-start(bf16[64,1024]{1,0:T(8,128)(2,1)S(1)} %get-tuple-element.20), channel_id=1, source_target_pairs={{0,64},{32,96},{64,0},{96,32},{1,65},{33,97},{65,1},{97,33},{2,66}... | collective-permute-start | bytes 393224 | tf_op jit(solution)/shard_map/ppermute | solution.py:242
  71.7 0.6 collective-permute-start.2
  72.3 0.0 collective-permute-done
  72.3 3.3 %collective-permute-done.1 = bf16[64,1024]{1,0:T(8,128)(2,1)S(1)} collective-permute-done((bf16[64,1024]{1,0:T(8,128)(2,1)S(1)}, bf16[64,1024]{1,0:T(8,128)(2,1)S(1)}, u32[]{:S(2)}, u32[]{:S(2)}) %collective-permute-start.1) | collective-permute-done | bytes 131104 | tf_op jit(solution)/shard_map/ppermute | solution.py:242
  75.6 3.0 %collective-permute-done.2 = bf16[64,1024]{1,0:T(8,128)(2,1)S(1)} collective-permute-done((bf16[64,1024]{1,0:T(8,128)(2,1)S(1)}, bf16[64,1024]{1,0:T(8,128)(2,1)S(1)}, u32[]{:S(2)}, u32[]{:S(2)}) %collective-permute-start.2) | collective-permute-done | bytes 131104 | tf_op jit(solution)/shard_map/ppermute | solution.py:242
  78.7 0.8 fusion.2
  79.5 0.0 all-to-all-done.1.data_ref
  79.5 0.0 copy-done.2
  79.5 0.0 copy-done.4
  79.5 1.8 %shard_map.123 = (bf16[128,2048]{1,0:T(8,128)(2,1)}, bf16[128,2048]{1,0:T(8,128)(2,1)}, bf16[128,2048]{1,0:T(8,128)(2,1)}) custom-call(bf16[32,128,128]{2,1,0:T(8,128)(2,1)S(1)} %all-to-all-done.1.data_ref, bf16[128,2048]{1,0:T(8,128)(2,1)S(1)} %bitcast.20, bf16[128,2048]{1,0:T(8,128)(2,1)S(1)} %bitcast.22, bf16[128,2048]{1,0:T(8,128)(2,1)S(1)} %bitcast.24), custom_call_target="tpu_custom_call" | custom-call | flops 2097152 | bytes 4194304 | tf_op jit(solution)/shard_map/pallas_call | solution.py:192
  (11 shorter events, 0.0 us)
Async XLA Ops:
  0.6 1.0 %copy-start.1 = (bf16[1,128,2048]{2,1,0:T(8,128)(2,1)S(1)}, bf16[1,128,2048]{2,1,0:T(8,128)(2,1)}, u32[]{:S(2)}) copy-start(bf16[1,128,2048]{2,1,0:T(8,128)(2,1)} %param.10) | copy-start | bytes 1572868
  1.7 1.0 %copy-start.3 = (bf16[1,128,2048]{2,1,0:T(8,128)(2,1)S(1)}, bf16[1,128,2048]{2,1,0:T(8,128)(2,1)}, u32[]{:S(2)}) copy-start(bf16[1,128,2048]{2,1,0:T(8,128)(2,1)} %param.11) | copy-start | bytes 1572868
  2.7 1.0 %copy-start.5 = (bf16[1,128,2048]{2,1,0:T(8,128)(2,1)S(1)}, bf16[1,128,2048]{2,1,0:T(8,128)(2,1)}, u32[]{:S(2)}) copy-start(bf16[1,128,2048]{2,1,0:T(8,128)(2,1)} %param.12) | copy-start | bytes 1572868
  3.8 1.0 %copy-start.12 = (bf16[1,128,2048]{2,1,0:T(8,128)(2,1)S(1)}, bf16[1,128,2048]{2,1,0:T(8,128)(2,1)}, u32[]{:S(2)}) copy-start(bf16[1,128,2048]{2,1,0:T(8,128)(2,1)} %param.9) | copy-start | bytes 1572868
  4.8 11.4 %copy-start.11 = (bf16[256,256]{1,0:T(8,128)(2,1)S(1)}, bf16[256,256]{1,0:T(8,128)(2,1)}, u32[]{:S(2)}) copy-start(bf16[256,256]{1,0:T(8,128)(2,1)} %constant.18.clone.ahead_ref) | copy-start | bytes 393220
  6.3 24.6 %copy-start.10 = (bf16[256,256]{1,0:T(8,128)(2,1)S(1)}, bf16[256,256]{1,0:T(8,128)(2,1)}, u32[]{:S(2)}) copy-start(bf16[256,256]{1,0:T(8,128)(2,1)} %constant.19.clone.back_ref) | copy-start | bytes 393220
  6.3 24.6 %all-to-all-start = ((bf16[32,128,128]{2,1,0:T(8,128)(2,1)}), bf16[32,128,128]{2,1,0:T(8,128)(2,1)S(1)}, u32[]{:S(2)}, u32[]{:S(2)}) async-start(bf16[32,128,128]{2,1,0:T(8,128)(2,1)} %shard_map.120), calls=%async_computation | async-start | bytes 2097152 | tf_op jit(solution)/shard_map/all_to_all | solution.py:221
  16.2 1.2 %copy-start.9 = (f32[64,4096]{1,0:T(8,128)S(1)}, f32[64,4096]{1,0:T(8,128)}, u32[]{:S(2)}) copy-start(f32[64,4096]{1,0:T(8,128)} %taps_ref.1) | copy-start | bytes 3145732
  25.5 1.3 %copy-start.7 = (f32[32,128,128]{2,1,0:T(8,128)}, f32[32,128,128]{2,1,0:T(8,128)S(1)}, u32[]{:S(2)}) copy-start(f32[32,128,128]{2,1,0:T(8,128)S(1)} %get-tuple-element.12.filt_im) | copy-start | bytes 6291460
  48.3 1.0 %copy-start.8 = (bf16[32,128,128]{2,1,0:T(8,128)(2,1)}, bf16[32,128,128]{2,1,0:T(8,128)(2,1)S(1)}, u32[]{:S(2)}) copy-start(bf16[32,128,128]{2,1,0:T(8,128)(2,1)S(1)} %get-tuple-element.13) | copy-start | bytes 3145732
  49.3 30.2 %all-to-all-start.1 = ((bf16[32,128,128]{2,1,0:T(8,128)(2,1)}), bf16[32,128,128]{2,1,0:T(8,128)(2,1)S(1)}, u32[]{:S(2)}, u32[]{:S(2)}) async-start(bf16[32,128,128]{2,1,0:T(8,128)(2,1)} %copy-done.8), calls=%async_computation.1 | async-start | bytes 2097152 | tf_op jit(solution)/shard_map/all_to_all | solution.py:229
  55.3 2.2 %copy-start = (f32[64,128,128]{2,1,0:T(8,128)S(1)}, f32[64,128,128]{2,1,0:T(8,128)}, u32[]{:S(2)}) copy-start(f32[64,128,128]{2,1,0:T(8,128)} %get-tuple-element.17.spec_ref) | copy-start | bytes 12582916
  57.5 22.0 %copy-start.2 = (bf16[1,128,2048]{2,1,0:T(8,128)(2,1)S(1)}, bf16[1,128,2048]{2,1,0:T(8,128)(2,1)}, u32[]{:S(2)}) copy-start(bf16[1,128,2048]{2,1,0:T(8,128)(2,1)} %param.10) | copy-start | bytes 1572868
  57.5 22.0 %copy-start.4 = (bf16[1,128,2048]{2,1,0:T(8,128)(2,1)S(1)}, bf16[1,128,2048]{2,1,0:T(8,128)(2,1)}, u32[]{:S(2)}) copy-start(bf16[1,128,2048]{2,1,0:T(8,128)(2,1)} %param.11) | copy-start | bytes 1572868
  57.5 22.0 %copy-start.6 = (bf16[1,128,2048]{2,1,0:T(8,128)(2,1)S(1)}, bf16[1,128,2048]{2,1,0:T(8,128)(2,1)}, u32[]{:S(2)}) copy-start(bf16[1,128,2048]{2,1,0:T(8,128)(2,1)} %param.12) | copy-start | bytes 1572868
  67.6 4.7 %collective-permute-start = (bf16[64,1024]{1,0:T(8,128)(2,1)S(1)}, bf16[64,1024]{1,0:T(8,128)(2,1)S(1)}, u32[]{:S(2)}, u32[]{:S(2)}) collective-permute-start(bf16[64,1024]{1,0:T(8,128)(2,1)S(1)} %get-tuple-element.18), channel_id=1, source_target_pairs={{0,32},{32,0},{64,96},{96,64},{1,33},{33,1},{65,97},{97,65},{2,34}... | collective-permute-start | bytes 393224 | tf_op jit(solution)/shard_map/ppermute | solution.py:242
  69.1 6.6 %collective-permute-start.1 = (bf16[64,1024]{1,0:T(8,128)(2,1)S(1)}, bf16[64,1024]{1,0:T(8,128)(2,1)S(1)}, u32[]{:S(2)}, u32[]{:S(2)}) collective-permute-start(bf16[64,1024]{1,0:T(8,128)(2,1)S(1)} %get-tuple-element.20), channel_id=1, source_target_pairs={{0,64},{32,96},{64,0},{96,32},{1,65},{33,97},{65,1},{97,33},{2,66}... | collective-permute-start | bytes 393224 | tf_op jit(solution)/shard_map/ppermute | solution.py:242
  71.7 7.0 %collective-permute-start.2 = (bf16[64,1024]{1,0:T(8,128)(2,1)S(1)}, bf16[64,1024]{1,0:T(8,128)(2,1)S(1)}, u32[]{:S(2)}, u32[]{:S(2)}) collective-permute-start(bf16[64,1024]{1,0:T(8,128)(2,1)S(1)} %get-tuple-element.19), channel_id=1, source_target_pairs={{0,96},{32,64},{64,32},{96,0},{1,97},{33,65},{65,33},{97,1},{2,98}... | collective-permute-start | bytes 393224 | tf_op jit(solution)/shard_map/ppermute | solution.py:242
where the time goes:
time: 81.9 us; the launch traced here: 81.3 us
  Pallas kernels  38.9 us (47%)
  starting transfers between devices  20.5 us (25%)
  waiting for transfers between devices  10.5 us (13%)
  local copies, waits for them, and re-layouts  9.92 us (12%)
    pallas_call x5, Pallas kernels, run(): pl.pallas_call(kernel, out_shape=out_shape, in_specs=[scalar] * smem + [i...  38.9 us
    unnamed x26, local copies, waits for them, and re-layouts  9.9 us
    all_to_all x1, starting transfers between devices, on_device(): data = lax.all_to_all(sent, 'seq', split_axis=0, concat_axis=0, tiled=True)  9.86 us
    ppermute x3, waiting for transfers between devices, on_device(): total = total + lax.ppermute(terms[shift], 'dp', pairs).astype(F32)  6.38 us
    all_to_all x1, starting transfers between devices, on_device(): lax.all_to_all(result, 'seq', split_axis=0, concat_axis=0, tiled=True)  5.96 us
    ppermute x3, starting transfers between devices, on_device(): total = total + lax.ppermute(terms[shift], 'dp', pairs).astype(F32)  4.72 us
    all_to_all x1, waiting for transfers between devices, on_device(): data = lax.all_to_all(sent, 'seq', split_axis=0, concat_axis=0, tiled=True)  4.08 us
  transfers between devices with their start and end apart: 5, of which 3 were waited for; matrix products, arithmetic and copies ran while one was open for 1% of the time, Pallas kernels for 22%

commit v1 on v0

v1 whole, which is shorter than its diff:
```python
import functools
import math

import jax
import jax.numpy as jnp
import ml_dtypes
import numpy as np
from jax import lax
from jax.experimental import pallas as pl
from jax.experimental.pallas import tpu as pltpu
from jax.sharding import PartitionSpec as P

TOKENS = 4096
ROWS = 32
COLS = 128
OWN = 64
SUB = 8
PAIR = 2 * SUB
BLOCK = ROWS * SUB
F32 = jnp.float32
BF16 = jnp.bfloat16
CHUNKS = 4
STEPS = OWN // PAIR
VMEM_LIMIT = 63 * 1024 * 1024


@functools.cache
def tables():
    index = np.arange(ROWS)
    rate = index + 0.25
    angle = 2.0 * np.pi * rate[:, None] * index[None, :] / ROWS
    parts = np.concatenate([np.cos(angle), -np.sin(angle)])
    first = np.kron(parts, np.eye(SUB))
    last = first.T / TOKENS
    twist = 2.0 * np.pi * rate[:, None] * np.arange(COLS)[None, :] / TOKENS
    turn = 2.0 * np.pi * (np.arange(COLS)[:, None] * np.arange(COLS)[None, :] % COLS) / COLS
    cos, sin = np.cos(turn), np.sin(turn)
    ahead = np.block([[cos, -sin], [sin, cos]])
    back = np.block([[cos, sin], [-sin, cos]])
    kind = ml_dtypes.bfloat16
    return (
        np.stack([np.cos(twist), np.sin(twist)]).astype(np.float32),
        first.astype(kind),
        ahead.astype(kind),
        last.astype(kind),
        back.astype(kind),
    )


def dot(left, right):
    return jnp.dot(left, right, preferred_element_type=F32)


def both(left, right):
    return jnp.concatenate([left, right], axis=1)


def split_rows(block):
    wide = block.astype(F32)
    low = wide[:, :SUB].reshape(BLOCK, COLS)
    high = wide[:, SUB:].reshape(BLOCK, COLS)
    return both(low, high).astype(BF16)


def tall(table):
    return jnp.broadcast_to(table[:, None, :], (ROWS, SUB, COLS)).reshape(BLOCK, COLS)


def spectrum(rows, twist_ref, first_ref, ahead_ref):
    cos, sin = tall(twist_ref[0]), tall(twist_ref[1])
    wide = dot(first_ref[...], rows)
    specs = []
    for side in range(2):
        lanes = slice(side * COLS, (side + 1) * COLS)
        real, imag = wide[:BLOCK, lanes], wide[BLOCK:, lanes]
        turned = both(real * cos + imag * sin, imag * cos - real * sin)
        specs.append(dot(turned.astype(BF16), ahead_ref[...]))
    return specs


def inverse(specs, twist_ref, last_ref, back_ref):
    cos, sin = tall(twist_ref[0]), tall(twist_ref[1])
    sides = []
    for spec in specs:
        wide = dot(spec.astype(BF16), back_ref[...])
        real, imag = wide[:, :COLS], wide[:, COLS:]
        sides.append(jnp.concatenate([real * cos - imag * sin, imag * cos + real * sin], axis=0))
    wide = dot(last_ref[...], both(*sides).astype(BF16))
    shape = (ROWS, SUB, COLS)
    return jnp.concatenate([wide[:, :COLS].reshape(shape), wide[:, COLS:].reshape(shape)], axis=1)


def product(left, right, conj):
    left_re, left_im = left[:, :COLS].astype(F32), left[:, COLS:].astype(F32)
    right_re, right_im = right[:, :COLS].astype(F32), right[:, COLS:].astype(F32)
    if conj:
        return both(left_re * right_re + left_im * right_im, left_re * right_im - left_im * right_re)
    return both(left_re * right_re - left_im * right_im, left_re * right_im + left_im * right_re)


def copies_of(pairs, sems):
    copies = []
    for place, (source, target) in enumerate(pairs):
        copies.append(pltpu.make_async_copy(source, target, sems.at[place]))
    for copy in copies:
        copy.start()
    return copies


def wait_all(copies):
    for copy in copies:
        copy.wait()


def gate_kernel(query_hbm, key_hbm, value_hbm, cotan_hbm, out_hbm, held, sent, in_sems, out_sems):
    sources = (key_hbm, value_hbm, query_hbm, cotan_hbm)
    span = held.shape[2] // CHUNKS
    pairs = []
    for chunk in range(CHUNKS):
        lanes = pl.ds(chunk * span, span)
        pairs += [(source.at[:, lanes], held.at[place, :, lanes]) for place, source in enumerate(sources)]
    arriving = copies_of(pairs, in_sems)
    leaving = []
    for chunk in range(CHUNKS):
        wait_all(arriving[4 * chunk : 4 * chunk + 4])
        first_block, last_block = chunk * span // COLS, (chunk + 1) * span // COLS
        for block in range(first_block, last_block):
            lanes = pl.ds(block * COLS, COLS)
            for part in range(2):
                left, right = held[2 * part, :, lanes].astype(F32), held[2 * part + 1, :, lanes].astype(F32)
                turned = (left * right).T.astype(BF16)
                rows = slice(part * OWN, (part + 1) * OWN)
                sent[2 * block, rows] = turned[:OWN]
                sent[2 * block + 1, rows] = turned[OWN:]
        dests = pl.ds(2 * first_block, 2 * (last_block - first_block))
        copy = pltpu.make_async_copy(sent.at[dests], out_hbm.at[dests], out_sems.at[chunk])
        copy.start()
        leaving.append(copy)
    wait_all(leaving)


def filter_kernel(
    taps_hbm, twist_hbm, first_hbm, ahead_hbm, out_hbm, taps, twist, first, ahead, filt, sems, out_sems
):
    pairs = [(first_hbm, first), (twist_hbm, twist), (ahead_hbm, ahead)]
    for step in range(STEPS):
        rows = pl.ds(step * PAIR, PAIR)
        pairs.append((taps_hbm.at[rows], taps.at[rows]))
    arriving = copies_of(pairs, sems)
    wait_all(arriving[:3])
    leaving = []
    for step in range(STEPS):
        arriving[3 + step].wait()
        sides = []
        for side in range(2):
            low = (2 * step + side) * SUB
            sides.append(
                jnp.concatenate([taps[low : low + SUB, p * COLS : (p + 1) * COLS] for p in range(ROWS)], axis=0)
            )
        specs = spectrum(both(*sides).astype(BF16), twist, first, ahead)
        for side in range(2):
            filt[2 * step + side] = specs[side].astype(BF16)
        groups = pl.ds(2 * step, 2)
        copy = pltpu.make_async_copy(filt.at[groups], out_hbm.at[groups], out_sems.at[step])
        copy.start()
        leaving.append(copy)
    wait_all(leaving)


def conv_kernel(
    data_hbm,
    filt_hbm,
    twist_hbm,
    first_hbm,
    ahead_hbm,
    last_hbm,
    back_hbm,
    out_hbm,
    cross_hbm,
    data,
    filt,
    twist,
    first,
    ahead,
    last,
    back,
    out,
    cross,
    sems,
    out_sems,
):
    pairs = [(first_hbm, first), (data_hbm, data), (twist_hbm, twist), (ahead_hbm, ahead)]
    pairs += [(filt_hbm, filt), (back_hbm, back), (last_hbm, last)]
    arriving = copies_of(pairs, sems)
    wait_all(arriving)
    leaving = []
    for step in range(STEPS):
        specs = []
        for part in range(2):
            rows = slice(part * OWN + step * PAIR, part * OWN + (step + 1) * PAIR)
            specs.append(spectrum(split_rows(data[:, rows, :]), twist, first, ahead))
        for part in range(2):
            rows = slice(part * OWN + step * PAIR, part * OWN + (step + 1) * PAIR)
            prods = [product(filt[2 * step + side], specs[part][side], part == 1) for side in range(2)]
            out[:, rows, :] = inverse(prods, twist, last, back).astype(BF16)
            leaving += copies_of([(out.at[:, rows, :], out_hbm.at[:, rows, :])], out_sems.at[step, part:])
        for side in range(2):
            cross[2 * step + side] = product(specs[0][side], specs[1][side], True).astype(BF16)
        groups = pl.ds(2 * step, 2)
        leaving += copies_of([(cross.at[groups], cross_hbm.at[groups])], out_sems.at[step, 2:])
    wait_all(leaving)


def taps_kernel(
    place_ref, cross_hbm, twist_hbm, last_hbm, back_hbm, own_hbm, near_hbm, cross, twist, last, back, lags_ref, sems, out_sems
):
    pairs = [(back_hbm, back), (cross_hbm, cross), (twist_hbm, twist), (last_hbm, last)]
    wait_all(copies_of(pairs, sems))
    per = ROWS // 4
    for step in range(STEPS):
        lags = inverse([cross[2 * step + side] for side in range(2)], twist, last, back).astype(BF16)
        rows = slice(step * PAIR, (step + 1) * PAIR)
        for p in range(ROWS):
            lags_ref[p // per, rows, (p % per) * COLS : (p % per + 1) * COLS] = lags[p]
    place = place_ref[0]
    pairs = []
    for shift in range(4):
        target = (own_hbm, near_hbm)[shift % 2]
        pairs.append((lags_ref.at[jnp.bitwise_xor(place, shift)], target.at[shift // 2]))
    wait_all(copies_of(pairs, out_sems))


def mix_kernel(
    data_hbm,
    key_hbm,
    value_hbm,
    cotan_hbm,
    own_hbm,
    near_hbm,
    far_hbm,
    query_out,
    key_out,
    value_out,
    filter_out,
    data,
    held,
    terms,
    grads,
    total,
    sems,
    out_sems,
):
    span = held.shape[2] // CHUNKS
    sources = (cotan_hbm, value_hbm, key_hbm)
    outs = (query_out, key_out, value_out)
    pairs = []
    for chunk in range(CHUNKS):
        dests = pl.ds(2 * chunk * span // COLS, 2 * span // COLS)
        lanes = pl.ds(chunk * span, span)
        pairs.append((data_hbm.at[dests], data.at[dests]))
        pairs += [(source.at[:, lanes], held.at[place, :, lanes]) for place, source in enumerate(sources)]
    pairs += [(source, terms.at[place]) for place, source in enumerate((own_hbm.at[0], near_hbm.at[0], far_hbm))]
    arriving = copies_of(pairs, sems)
    leaving = []
    for chunk in range(CHUNKS):
        wait_all(arriving[4 * chunk : 4 * chunk + 4])
        for block in range(chunk * span // COLS, (chunk + 1) * span // COLS):
            lanes = pl.ds(block * COLS, COLS)
            turned = []
            for part in range(2):
                rows = slice(part * OWN, (part + 1) * OWN)
                tall = jnp.concatenate([data[2 * block, rows], data[2 * block + 1, rows]], axis=0)
                turned.append(tall.astype(F32).T)
            conv, grad = turned
            for place, factor in enumerate((conv, grad, grad)):
                grads[place, :, lanes] = (factor * held[place, :, lanes].astype(F32)).astype(BF16)
        lanes = pl.ds(chunk * span, span)
        pairs = [(grads.at[place, :, lanes], outs[place].at[:, lanes]) for place in range(3)]
        leaving += copies_of(pairs, out_sems.at[chunk])
    wait_all(arriving[4 * CHUNKS :])
    whole = terms[0].astype(F32) + terms[1].astype(F32) + terms[2].astype(F32)
    total[...] = whole * (1.0 / math.sqrt(4 * TOKENS))
    leaving += copies_of([(total, filter_out)], out_sems.at[CHUNKS])
    wait_all(leaving)


def call(kernel, out_shape, scratch=(), flops=0, nbytes=0, smem=0):
    far = pl.BlockSpec(memory_space=pl.ANY)
    scalar = pl.BlockSpec(memory_space=pltpu.SMEM)

    def run(*args):
        return pl.pallas_call(
            kernel,
            out_shape=out_shape,
            in_specs=[scalar] * smem + [far] * (len(args) - smem),
            out_specs=jax.tree.map(lambda _: far, out_shape),
            scratch_shapes=list(scratch),
            compiler_params=pltpu.CompilerParams(vmem_limit_bytes=VMEM_LIMIT),
            cost_estimate=pl.CostEstimate(flops=flops, bytes_accessed=nbytes, transcendentals=0),
        )(*args)

    return run


def swap(array):
    return lax.all_to_all(array, "seq", split_axis=0, concat_axis=0, tiled=True)


def on_device(query_in, key_in, value_in, grad_out, filter_taps):
    twist, first, ahead, last, back = (jnp.asarray(table) for table in tables())
    query, keys, values, cotan = query_in[0], key_in[0], value_in[0], grad_out[0]
    shape = jax.ShapeDtypeStruct
    sems = pltpu.SemaphoreType.DMA
    cube = shape((ROWS, 2 * OWN, COLS), BF16)
    filt_spec = shape((OWN // SUB, BLOCK, 2 * COLS), BF16)
    wide = shape(query.shape, BF16)
    quarter = shape((OWN, TOKENS // 4), BF16)
    unit = 1 << 30

    def room(*arrays):
        return [pltpu.VMEM(array.shape, array.dtype) for array in arrays]

    sent = call(
        gate_kernel,
        cube,
        [pltpu.VMEM((4, *query.shape), BF16), *room(cube), sems((4 * CHUNKS,)), sems((CHUNKS,))],
        flops=1 << 20,
        nbytes=3 << 20,
    )(query, keys, values, cotan)
    filt = call(
        filter_kernel,
        filt_spec,
        [*room(filter_taps, twist, first, ahead, filt_spec), sems((3 + STEPS,)), sems((STEPS,))],
        flops=unit // 2,
        nbytes=3 << 20,
    )(filter_taps, twist, first, ahead)
    data = swap(sent)
    result, cross = call(
        conv_kernel,
        (cube, filt_spec),
        [
            *room(cube, filt_spec, twist, first, ahead, last, back, cube, filt_spec),
            sems((7,)),
            sems((STEPS, 3)),
        ],
        flops=2 * unit,
        nbytes=5 << 20,
    )(data, filt, twist, first, ahead, last, back)
    returned = swap(result)
    place = lax.axis_index("dp").astype(jnp.int32).reshape(1)
    half = shape((2, *quarter.shape), BF16)
    own, sent_near = call(
        taps_kernel,
        (half, half),
        [
            *room(filt_spec, twist, last, back),
            pltpu.VMEM((4, *quarter.shape), BF16),
            sems((4,)),
            sems((4,)),
        ],
        flops=unit // 2,
        nbytes=2 << 20,
        smem=1,
    )(place, cross, twist, last, back)
    near = lax.ppermute(sent_near, "dp", [(d, d ^ 1) for d in range(4)])
    partial = (own[1].astype(F32) + near[1].astype(F32)).astype(BF16)
    far = lax.ppermute(partial, "dp", [(d, d ^ 2) for d in range(4)])
    grad_query, grad_key, grad_value, grad_filter = call(
        mix_kernel,
        (wide, wide, wide, shape(quarter.shape, F32)),
        [
            *room(cube),
            pltpu.VMEM((3, *wide.shape), BF16),
            pltpu.VMEM((3, *quarter.shape), BF16),
            pltpu.VMEM((3, *wide.shape), BF16),
            pltpu.VMEM(quarter.shape, F32),
            sems((4 * CHUNKS + 3,)),
            sems((CHUNKS + 1, 3)),
        ],
        flops=1 << 20,
        nbytes=4 << 20,
    )(returned, keys, values, cotan, own, near, far)
    return (grad_query[None], grad_key[None], grad_value[None], grad_filter)


def solution(mesh):
    tokens = P("dp", "seq", None)
    return jax.shard_map(
        on_device,
        mesh=mesh,
        in_specs=(tokens, tokens, tokens, tokens, P("seq", None)),
        out_specs=(tokens, tokens, tokens, P("seq", "dp")),
        check_vma=False,
    )
```

time: 81.9 us -> 63 us (0.77)
  Pallas kernels: 38.9 us -> 19 us
  waiting for transfers between devices: 10.5 us -> 21 us
  local copies, waits for them, and re-layouts: 9.92 us -> 0.65 us
    pallas_call x5, Pallas kernels: 38.9 us -> 19 us  [run(): pl.pallas_call(kernel, out_shape=out_shape, in_specs=[scalar] * smem + [f...]
    unnamed x26 -> x4, local copies, waits for them, and re-layouts: 9.9 us -> 0.65 us
    all_to_all x2, waiting for transfers between devices: 4.09 us -> 10.9 us  [swap(): return lax.all_to_all(array, 'seq', split_axis=0, concat_axis=0, tiled=True)]
    ppermute x3 -> x2, waiting for transfers between devices: 6.38 us -> 10.1 us  [the longest x1 8.7 us: on_device(): far = lax.ppermute(partial, 'dp', [(d, d ^ 2) for d in range(4)])]
    convert_element_type x0 -> x1, other arithmetic: none -> 1.03 us  [on_device(): partial = (own[1].astype(F32) + near[1].astype(F32)).astype(BF16)]
    ppermute x3 -> x2, starting transfers between devices: 4.72 us -> 4.24 us  [the longest x1 2.7 us: on_device(): far = lax.ppermute(partial, 'dp', [(d, d ^ 2) for d in range(4)])]
  transfers between devices with their start and end apart: 5 -> 4, of which waited for: 3 -> 3; matrix products, arithmetic and copies ran while one was open for 1% -> 2% of each run, Pallas kernels for 22% -> 11%
where the time goes in v1:
time: 63 us; the launch traced here: 62.5 us
  waiting for transfers between devices  21 us (33%)
  starting transfers between devices  20.2 us (32%)
  Pallas kernels  19 us (30%)
  other arithmetic  1.03 us (2%)
  between operations  0.69 us (1%)
  local copies, waits for them, and re-layouts  0.65 us (1%)
    pallas_call x5, Pallas kernels, run(): pl.pallas_call(kernel, out_shape=out_shape, in_specs=[scalar] * smem + [f...  19 us
    all_to_all x2, starting transfers between devices, swap(): return lax.all_to_all(array, 'seq', split_axis=0, concat_axis=0, tiled=True)  15.9 us
    all_to_all x2, waiting for transfers between devices, swap(): return lax.all_to_all(array, 'seq', split_axis=0, concat_axis=0, tiled=True)  10.9 us
    ppermute x1, waiting for transfers between devices, on_device(): far = lax.ppermute(partial, 'dp', [(d, d ^ 2) for d in range(4)])  8.7 us
    ppermute x1, starting transfers between devices, on_device(): far = lax.ppermute(partial, 'dp', [(d, d ^ 2) for d in range(4)])  2.7 us
    ppermute x1, starting transfers between devices, on_device(): near = lax.ppermute(sent_near, 'dp', [(d, d ^ 1) for d in range(4)])  1.53 us
    ppermute x1, waiting for transfers between devices, on_device(): near = lax.ppermute(sent_near, 'dp', [(d, d ^ 1) for d in range(4)])  1.37 us
  transfers between devices with their start and end apart: 4, of which 3 were waited for; matrix products, arithmetic and copies ran while one was open for 2% of the time, Pallas kernels for 11%

profile of v1, /device:TPU:1, one launch (start us, length us, event | category | flops | bytes accessed | tf_op | source)
XLA Modules:
  0.0 62.5 jit_solution(3892000819049352505)
XLA Ops:
  0.6 2.6 %shard_map.129 = bf16[32,128,128]{2,1,0:T(8,128)(2,1)} custom-call(bf16[128,2048]{1,0:T(8,128)(2,1)} %bitcast.16, bf16[128,2048]{1,0:T(8,128)(2,1)} %bitcast.10, bf16[128,2048]{1,0:T(8,128)(2,1)} %bitcast.12, bf16[128,2048]{1,0:T(8,128)(2,1)} %bitcast.14), custom_call_target="tpu_custom_call" | custom-call | flops 1048576 | bytes 3145728 | tf_op jit(solution)/shard_map/pallas_call | solution.py:292
  3.3 9.9 %all-to-all-start = ((bf16[32,128,128]{2,1,0:T(8,128)(2,1)}), bf16[32,128,128]{2,1,0:T(8,128)(2,1)}, u32[]{:S(2)}, u32[]{:S(2)}) async-start(bf16[32,128,128]{2,1,0:T(8,128)(2,1)} %shard_map.129), calls=%async_computation | async-start | bytes 2097152 | tf_op jit(solution)/shard_map/all_to_all | solution.py:306
  13.1 3.8 %shard_map.130.filt_hbm = bf16[8,256,256]{2,1,0:T(8,128)(2,1)} custom-call(f32[64,4096]{1,0:T(8,128)} %taps_hbm.1, f32[2,32,128]{2,1,0:T(8,128)} %constant.16.clone.twist_hbm, bf16[512,256]{1,0:T(8,128)(2,1)} %constant.17.clone.first_hbm, bf16[256,256]{1,0:T(8,128)(2,1)} %constant.18.clone.ahead_hbm), custom_call_target="tpu_custom_call" | custom-call | flops 536870912 | bytes 3145728 | tf_op jit(solution)/shard_map/pallas_call | solution.py:292
  16.9 10.9 %all-to-all-done.data_hbm = bf16[32,128,128]{2,1,0:T(8,128)(2,1)} async-done(((bf16[32,128,128]{2,1,0:T(8,128)(2,1)}), bf16[32,128,128]{2,1,0:T(8,128)(2,1)}, u32[]{:S(2)}, u32[]{:S(2)}) %all-to-all-start) | async-done | bytes 1048608 | tf_op jit(solution)/shard_map/all_to_all | solution.py:306
  27.8 6.4 %shard_map.131 = (bf16[32,128,128]{2,1,0:T(8,128)(2,1)}, bf16[8,256,256]{2,1,0:T(8,128)(2,1)}) custom-call(bf16[32,128,128]{2,1,0:T(8,128)(2,1)} %all-to-all-done.data_hbm, bf16[8,256,256]{2,1,0:T(8,128)(2,1)} %shard_map.130.filt_hbm, f32[2,32,128]{2,1,0:T(8,128)} %constant.16.clone.twist_hbm, bf16[512,256]{1,0:T(8,128)(2,1)} %constant.17.clone.first_hbm, ...), custom_call_target="tpu_custom_call" | custom-call | flops 2147483648 | bytes 5242880 | tf_op jit(solution)/shard_map/pallas_call | solution.py:292
  34.2 6.1 %all-to-all-start.1 = ((bf16[32,128,128]{2,1,0:T(8,128)(2,1)}), bf16[32,128,128]{2,1,0:T(8,128)(2,1)}, u32[]{:S(2)}, u32[]{:S(2)}) async-start(bf16[32,128,128]{2,1,0:T(8,128)(2,1)} %get-tuple-element.12), calls=%async_computation.1 | async-start | bytes 2097152 | tf_op jit(solution)/shard_map/all_to_all | solution.py:306
  40.3 3.2 %shard_map.132 = (bf16[2,64,1024]{2,1,0:T(8,128)(2,1)}, bf16[2,64,1024]{2,1,0:T(8,128)(2,1)}) custom-call(s32[1]{0:T(128)} %bitcast.4.place_ref, bf16[8,256,256]{2,1,0:T(8,128)(2,1)} %get-tuple-element.13.cross_hbm, f32[2,32,128]{2,1,0:T(8,128)} %constant.16.clone.twist_hbm, bf16[256,512]{1,0:T(8,128)(2,1)} %constant.19.clone.last_hbm, ...), custom_call_target="tpu_custom_call" | custom-call | flops 536870912 | bytes 2097152 | tf_op jit(solution)/shard_map/pallas_call | solution.py:292
  43.5 1.5 %collective-permute-start = (bf16[2,64,1024]{2,1,0:T(8,128)(2,1)}, bf16[2,64,1024]{2,1,0:T(8,128)(2,1)S(1)}, u32[]{:S(2)}, u32[]{:S(2)}) collective-permute-start(bf16[2,64,1024]{2,1,0:T(8,128)(2,1)} %get-tuple-element.15), channel_id=1, source_target_pairs={{0,32},{32,0},{64,96},{96,64},{1,33},{33,1},{65,97},{97,65},{2,34}... | collective-permute-start | bytes 786440 | tf_op jit(solution)/shard_map/ppermute | solution.py:365
  45.0 1.4 %collective-permute-done.near_hbm = bf16[2,64,1024]{2,1,0:T(8,128)(2,1)S(1)} collective-permute-done((bf16[2,64,1024]{2,1,0:T(8,128)(2,1)}, bf16[2,64,1024]{2,1,0:T(8,128)(2,1)S(1)}, u32[]{:S(2)}, u32[]{:S(2)}) %collective-permute-start) | collective-permute-done | bytes 262176 | tf_op jit(solution)/shard_map/ppermute | solution.py:365
  46.4 0.0 copy-start
  46.4 1.0 %fusion = bf16[64,1024]{1,0:T(8,128)(2,1)S(1)} fusion(bf16[2,64,1024]{2,1,0:T(8,128)(2,1)S(1)} %collective-permute-done.near_hbm, bf16[2,64,1024]{2,1,0:T(8,128)(2,1)} %get-tuple-element.14.own_hbm), kind=kLoop, calls=%fused_computation.1 | loop fusion | flops 262144 | bytes 393216 | tf_op jit(solution)/shard_map/convert_element_type | solution.py:366
  47.4 2.7 %collective-permute-start.1 = (bf16[64,1024]{1,0:T(8,128)(2,1)S(1)}, bf16[64,1024]{1,0:T(8,128)(2,1)S(1)}, u32[]{:S(2)}, u32[]{:S(2)}) collective-permute-start(bf16[64,1024]{1,0:T(8,128)(2,1)S(1)} %fusion), channel_id=1, source_target_pairs={{0,64},{32,96},{64,0},{96,32},{1,65},{33,97},{65,1},{97,33},{2,66}... | collective-permute-start | bytes 393224 | tf_op jit(solution)/shard_map/ppermute | solution.py:367
  50.1 8.7 %collective-permute-done.1.far_hbm = bf16[64,1024]{1,0:T(8,128)(2,1)S(1)} collective-permute-done((bf16[64,1024]{1,0:T(8,128)(2,1)S(1)}, bf16[64,1024]{1,0:T(8,128)(2,1)S(1)}, u32[]{:S(2)}, u32[]{:S(2)}) %collective-permute-start.1) | collective-permute-done | bytes 131104 | tf_op jit(solution)/shard_map/ppermute | solution.py:367
  58.8 0.0 copy-start.1
  58.8 0.0 all-to-all-done.1.data_hbm
  58.8 0.0 copy-done
  58.8 0.6 %copy-done.1 = bf16[64,1024]{1,0:T(8,128)(2,1)} copy-done((bf16[64,1024]{1,0:T(8,128)(2,1)}, bf16[64,1024]{1,0:T(8,128)(2,1)S(1)}, u32[]{:S(2)}) %copy-start.1) | copy-done | bytes 131096
  59.5 3.0 %shard_map.133 = (bf16[128,2048]{1,0:T(8,128)(2,1)}, bf16[128,2048]{1,0:T(8,128)(2,1)}, bf16[128,2048]{1,0:T(8,128)(2,1)}, f32[64,1024]{1,0:T(8,128)}) custom-call(bf16[32,128,128]{2,1,0:T(8,128)(2,1)} %all-to-all-done.1.data_hbm, bf16[128,2048]{1,0:T(8,128)(2,1)} %bitcast.11, bf16[128,2048]{1,0:T(8,128)(2,1)} %bitcast.13, bf16[128,2048]{1,0:T(8,128)(2,1)} %bitcast.15, ...), custom_call_target="tpu_custom_call" | custom-call | flops 1048576 | bytes 4194304 | tf_op jit(solution)/shard_map/pallas_call | solution.py:292
Async XLA Ops:
  3.3 24.6 %all-to-all-start = ((bf16[32,128,128]{2,1,0:T(8,128)(2,1)}), bf16[32,128,128]{2,1,0:T(8,128)(2,1)}, u32[]{:S(2)}, u32[]{:S(2)}) async-start(bf16[32,128,128]{2,1,0:T(8,128)(2,1)} %shard_map.129), calls=%async_computation | async-start | bytes 2097152 | tf_op jit(solution)/shard_map/all_to_all | solution.py:306
  34.2 24.6 %all-to-all-start.1 = ((bf16[32,128,128]{2,1,0:T(8,128)(2,1)}), bf16[32,128,128]{2,1,0:T(8,128)(2,1)}, u32[]{:S(2)}, u32[]{:S(2)}) async-start(bf16[32,128,128]{2,1,0:T(8,128)(2,1)} %get-tuple-element.12), calls=%async_computation.1 | async-start | bytes 2097152 | tf_op jit(solution)/shard_map/all_to_all | solution.py:306
  43.5 2.9 %collective-permute-start = (bf16[2,64,1024]{2,1,0:T(8,128)(2,1)}, bf16[2,64,1024]{2,1,0:T(8,128)(2,1)S(1)}, u32[]{:S(2)}, u32[]{:S(2)}) collective-permute-start(bf16[2,64,1024]{2,1,0:T(8,128)(2,1)} %get-tuple-element.15), channel_id=1, source_target_pairs={{0,32},{32,0},{64,96},{96,64},{1,33},{33,1},{65,97},{97,65},{2,34}... | collective-permute-start | bytes 786440 | tf_op jit(solution)/shard_map/ppermute | solution.py:365
  46.4 12.5 %copy-start = (bf16[2,64,1024]{2,1,0:T(8,128)(2,1)}, bf16[2,64,1024]{2,1,0:T(8,128)(2,1)S(1)}, u32[]{:S(2)}) copy-start(bf16[2,64,1024]{2,1,0:T(8,128)(2,1)S(1)} %collective-permute-done.near_hbm) | copy-start | bytes 786436
  47.4 11.4 %collective-permute-start.1 = (bf16[64,1024]{1,0:T(8,128)(2,1)S(1)}, bf16[64,1024]{1,0:T(8,128)(2,1)S(1)}, u32[]{:S(2)}, u32[]{:S(2)}) collective-permute-start(bf16[64,1024]{1,0:T(8,128)(2,1)S(1)} %fusion), channel_id=1, source_target_pairs={{0,64},{32,96},{64,0},{96,32},{1,65},{33,97},{65,1},{97,33},{2,66}... | collective-permute-start | bytes 393224 | tf_op jit(solution)/shard_map/ppermute | solution.py:367
  58.8 0.7 %copy-start.1 = (bf16[64,1024]{1,0:T(8,128)(2,1)}, bf16[64,1024]{1,0:T(8,128)(2,1)S(1)}, u32[]{:S(2)}) copy-start(bf16[64,1024]{1,0:T(8,128)(2,1)S(1)} %collective-permute-done.1.far_hbm) | copy-start | bytes 393220

commit v2 on v1

v2 whole, which is shorter than its diff:
```python
import functools
import math

import jax
import jax.numpy as jnp
import ml_dtypes
import numpy as np
from jax import lax
from jax.experimental import pallas as pl
from jax.experimental.pallas import tpu as pltpu
from jax.sharding import PartitionSpec as P

TOKENS = 4096
ROWS = 32
COLS = 128
OWN = 64
SUB = 8
PAIR = 2 * SUB
BLOCK = ROWS * SUB
F32 = jnp.float32
BF16 = jnp.bfloat16
CHUNKS = 4
STEPS = OWN // PAIR
VMEM_LIMIT = 24 * 1024 * 1024


@functools.cache
def tables():
    index = np.arange(ROWS)
    rate = index + 0.25
    angle = 2.0 * np.pi * rate[:, None] * index[None, :] / ROWS
    parts = np.concatenate([np.cos(angle), -np.sin(angle)])
    first = np.kron(parts, np.eye(SUB))
    last = first.T / TOKENS
    twist = 2.0 * np.pi * rate[:, None] * np.arange(COLS)[None, :] / TOKENS
    turn = 2.0 * np.pi * (np.arange(COLS)[:, None] * np.arange(COLS)[None, :] % COLS) / COLS
    cos, sin = np.cos(turn), np.sin(turn)
    ahead = np.block([[cos, -sin], [sin, cos]])
    back = np.block([[cos, sin], [-sin, cos]])
    kind = ml_dtypes.bfloat16
    return (
        np.stack([np.cos(twist), np.sin(twist)]).astype(np.float32),
        first.astype(kind),
        ahead.astype(kind),
        last.astype(kind),
        back.astype(kind),
    )


def dot(left, right):
    return jnp.dot(left, right, preferred_element_type=F32)


def both(left, right):
    return jnp.concatenate([left, right], axis=1)


def split_rows(block):
    wide = block.astype(F32)
    low = wide[:, :SUB].reshape(BLOCK, COLS)
    high = wide[:, SUB:].reshape(BLOCK, COLS)
    return both(low, high).astype(BF16)


def turns(twist_ref):
    spread = [jnp.broadcast_to(twist_ref[i][:, None, :], (ROWS, SUB, COLS)) for i in range(2)]
    return [table.reshape(BLOCK, COLS) for table in spread]


def spectra(blocks, twist_ref, first_ref, ahead_ref):
    cos, sin = turns(twist_ref)
    turned = []
    for rows in blocks:
        wide = dot(first_ref[...], rows)
        for side in range(2):
            lanes = slice(side * COLS, (side + 1) * COLS)
            real, imag = wide[:BLOCK, lanes], wide[BLOCK:, lanes]
            turned.append(both(real * cos + imag * sin, imag * cos - real * sin).astype(BF16))
    return dot(jnp.concatenate(turned, axis=0), ahead_ref[...])


def unturned(specs, twist_ref, back_ref):
    cos, sin = turns(twist_ref)
    wide = dot(specs.astype(BF16), back_ref[...])
    blocks = []
    for place in range(specs.shape[0] // (2 * BLOCK)):
        sides = []
        for side in range(2):
            low = (2 * place + side) * BLOCK
            real, imag = wide[low : low + BLOCK, :COLS], wide[low : low + BLOCK, COLS:]
            sides.append(jnp.concatenate([real * cos - imag * sin, imag * cos + real * sin], axis=0))
        blocks.append(both(*sides).astype(BF16))
    return blocks


def lags_of(rows, last_ref):
    wide = dot(last_ref[...], rows)
    shape = (ROWS, SUB, COLS)
    return jnp.concatenate([wide[:, :COLS].reshape(shape), wide[:, COLS:].reshape(shape)], axis=1)


def product(left, right, conj):
    left_re, left_im = left[:, :COLS].astype(F32), left[:, COLS:].astype(F32)
    right_re, right_im = right[:, :COLS].astype(F32), right[:, COLS:].astype(F32)
    if conj:
        return both(left_re * right_re + left_im * right_im, left_re * right_im - left_im * right_re)
    return both(left_re * right_re - left_im * right_im, left_re * right_im + left_im * right_re)


def copies_of(pairs, sems):
    copies = []
    for place, (source, target) in enumerate(pairs):
        copies.append(pltpu.make_async_copy(source, target, sems.at[place]))
    for copy in copies:
        copy.start()
    return copies


def wait_all(copies):
    for copy in copies:
        copy.wait()


def gate_kernel(query_hbm, key_hbm, value_hbm, cotan_hbm, out_hbm, held, sent, in_sems, out_sems):
    sources = (key_hbm, value_hbm, query_hbm, cotan_hbm)
    span = held.shape[2] // CHUNKS
    pairs = []
    for chunk in range(CHUNKS):
        lanes = pl.ds(chunk * span, span)
        pairs += [(source.at[:, lanes], held.at[place, :, lanes]) for place, source in enumerate(sources)]
    arriving = copies_of(pairs, in_sems)
    leaving = []
    for chunk in range(CHUNKS):
        wait_all(arriving[4 * chunk : 4 * chunk + 4])
        first_block, last_block = chunk * span // COLS, (chunk + 1) * span // COLS
        for block in range(first_block, last_block):
            lanes = pl.ds(block * COLS, COLS)
            for part in range(2):
                left, right = held[2 * part, :, lanes].astype(F32), held[2 * part + 1, :, lanes].astype(F32)
                turned = (left * right).T.astype(BF16)
                rows = slice(part * OWN, (part + 1) * OWN)
                sent[2 * block, rows] = turned[:OWN]
                sent[2 * block + 1, rows] = turned[OWN:]
        dests = pl.ds(2 * first_block, 2 * (last_block - first_block))
        copy = pltpu.make_async_copy(sent.at[dests], out_hbm.at[dests], out_sems.at[chunk])
        copy.start()
        leaving.append(copy)
    wait_all(leaving)


def filter_kernel(
    taps_hbm,
    twist_hbm,
    first_hbm,
    ahead_hbm,
    last_hbm,
    back_hbm,
    filt,
    twist,
    first,
    ahead,
    last,
    back,
    taps,
    sems,
):
    pairs = [(first_hbm, first), (twist_hbm, twist), (ahead_hbm, ahead), (taps_hbm, taps)]
    pairs += [(last_hbm, last), (back_hbm, back)]
    arriving = copies_of(pairs, sems)
    wait_all(arriving[:4])
    for step in range(STEPS):
        sides = []
        for side in range(2):
            low = (2 * step + side) * SUB
            sides.append(
                jnp.concatenate([taps[low : low + SUB, p * COLS : (p + 1) * COLS] for p in range(ROWS)], axis=0)
            )
        filt[step] = spectra([both(*sides).astype(BF16)], twist, first, ahead).astype(BF16)
    wait_all(arriving[4:])


def conv_kernel(data, filt, twist, first, ahead, last, back, out_hbm, cross_hbm, out, cross, out_sems):
    leaving = []
    for step in range(STEPS):
        blocks = []
        for part in range(2):
            rows = slice(part * OWN + step * PAIR, part * OWN + (step + 1) * PAIR)
            blocks.append(split_rows(data[:, rows, :]))
        specs = spectra(blocks, twist, first, ahead)
        gated, grads, turn = specs[: 2 * BLOCK], specs[2 * BLOCK :], filt[step]
        cross[step] = product(gated, grads, True).astype(BF16)
        leaving += copies_of([(cross.at[step], cross_hbm.at[step])], out_sems.at[step, 2:])
        prods = jnp.concatenate([product(turn, gated, False), product(turn, grads, True)], axis=0)
        for part, block in enumerate(unturned(prods, twist, back)):
            rows = slice(part * OWN + step * PAIR, part * OWN + (step + 1) * PAIR)
            out[:, rows, :] = lags_of(block, last).astype(BF16)
            leaving += copies_of([(out.at[:, rows, :], out_hbm.at[:, rows, :])], out_sems.at[step, part:])
    wait_all(leaving)


def taps_kernel(
    place_ref,
    cross_hbm,
    key_hbm,
    value_hbm,
    cotan_hbm,
    twist,
    last,
    back,
    own,
    near,
    keys,
    values,
    cotan,
    cross,
    lags_ref,
    sems,
    out_sems,
):
    pairs = [(cross_hbm, cross), (key_hbm, keys), (value_hbm, values), (cotan_hbm, cotan)]
    arriving = copies_of(pairs, sems)
    arriving[0].wait()
    per = ROWS // 4
    for step in range(STEPS):
        lags = lags_of(unturned(cross[step], twist, back)[0], last).astype(BF16)
        rows = slice(step * PAIR, (step + 1) * PAIR)
        for p in range(ROWS):
            lags_ref[p // per, rows, (p % per) * COLS : (p % per + 1) * COLS] = lags[p]
    place = place_ref[0]
    pairs = []
    for shift in range(4):
        target = (own, near)[shift % 2]
        pairs.append((lags_ref.at[jnp.bitwise_xor(place, shift)], target.at[shift // 2]))
    wait_all(copies_of(pairs, out_sems))
    wait_all(arriving[1:])


def mix_kernel(
    data, near, far, own, keys, values, cotan, query_out, key_out, value_out, filter_out, grads, total, out_sems
):
    span = keys.shape[1] // CHUNKS
    factors = (cotan, values, keys)
    outs = (query_out, key_out, value_out)
    whole = own[0].astype(F32) + near[0].astype(F32) + far[...].astype(F32)
    total[...] = whole * (1.0 / math.sqrt(4 * TOKENS))
    leaving = copies_of([(total, filter_out)], out_sems.at[CHUNKS])
    for chunk in range(CHUNKS):
        for block in range(chunk * span // COLS, (chunk + 1) * span // COLS):
            lanes = pl.ds(block * COLS, COLS)
            turned = []
            for part in range(2):
                rows = slice(part * OWN, (part + 1) * OWN)
                tall = jnp.concatenate([data[2 * block, rows], data[2 * block + 1, rows]], axis=0)
                turned.append(tall.astype(F32).T)
            conv, grad = turned
            for place, turn in enumerate((conv, grad, grad)):
                grads[place, :, lanes] = (turn * factors[place][:, lanes].astype(F32)).astype(BF16)
        lanes = pl.ds(chunk * span, span)
        pairs = [(grads.at[place, :, lanes], outs[place].at[:, lanes]) for place in range(3)]
        leaving += copies_of(pairs, out_sems.at[chunk])
    wait_all(leaving)


def call(kernel, out_shape, places, scratch=(), flops=0, nbytes=0):
    spaces = {"h": pltpu.HBM, "v": pltpu.VMEM, "s": pltpu.SMEM}
    specs = {"h": pl.BlockSpec(memory_space=pl.ANY)}
    specs |= {place: pl.BlockSpec(memory_space=spaces[place]) for place in "vs"}
    ins, outs = places.split()

    def run(*args):
        held = [pltpu.with_memory_space_constraint(x, spaces[p]) if p != "s" else x for x, p in zip(args, ins, strict=True)]
        return pl.pallas_call(
            kernel,
            out_shape=tuple(spaces[p](x.shape, x.dtype) for x, p in zip(out_shape, outs, strict=True)),
            in_specs=[specs[p] for p in ins],
            out_specs=tuple(specs[p] for p in outs),
            scratch_shapes=list(scratch),
            compiler_params=pltpu.CompilerParams(vmem_limit_bytes=VMEM_LIMIT),
            cost_estimate=pl.CostEstimate(flops=flops, bytes_accessed=nbytes, transcendentals=0),
        )(*held)

    return run


def swap(array):
    return lax.all_to_all(array, "seq", split_axis=0, concat_axis=0, tiled=True)


def on_device(query_in, key_in, value_in, grad_out, filter_taps):
    twist, first, ahead, last, back = (jnp.asarray(table) for table in tables())
    query, keys, values, cotan = query_in[0], key_in[0], value_in[0], grad_out[0]
    shape = jax.ShapeDtypeStruct
    sems = pltpu.SemaphoreType.DMA
    cube = shape((ROWS, 2 * OWN, COLS), BF16)
    filt_spec = shape((STEPS, 2 * BLOCK, 2 * COLS), BF16)
    wide = shape(query.shape, BF16)
    quarter = shape((OWN, TOKENS // 4), BF16)
    unit = 1 << 30

    def room(*arrays):
        return [pltpu.VMEM(array.shape, array.dtype) for array in arrays]

    (sent,) = call(
        gate_kernel,
        (cube,),
        "hhhh h",
        [pltpu.VMEM((4, *query.shape), BF16), *room(cube), sems((4 * CHUNKS,)), sems((CHUNKS,))],
        flops=1 << 20,
        nbytes=3 << 20,
    )(query, keys, values, cotan)
    filt, twist, first, ahead, last, back = call(
        filter_kernel,
        (filt_spec, twist, first, ahead, last, back),
        "hhhhhh vvvvvv",
        [*room(filter_taps), sems((6,))],
        flops=unit // 2,
        nbytes=3 << 20,
    )(filter_taps, twist, first, ahead, last, back)
    data = swap(sent)
    result, cross = call(
        conv_kernel,
        (cube, filt_spec),
        "vvvvvvv hh",
        [*room(cube, filt_spec), sems((STEPS, 3))],
        flops=2 * unit,
        nbytes=5 << 20,
    )(data, filt, twist, first, ahead, last, back)
    returned = swap(result)
    place = lax.axis_index("dp").astype(jnp.int32).reshape(1)
    half = shape((2, *quarter.shape), BF16)
    own, sent_near, keys, values, cotan = call(
        taps_kernel,
        (half, half, wide, wide, wide),
        "shhhhvvv vvvvv",
        [*room(filt_spec), pltpu.VMEM((4, *quarter.shape), BF16), sems((4,)), sems((4,))],
        flops=unit // 2,
        nbytes=3 << 20,
    )(place, cross, keys, values, cotan, twist, last, back)
    near = lax.ppermute(sent_near, "dp", [(d, d ^ 1) for d in range(4)])
    partial = (own[1].astype(F32) + near[1].astype(F32)).astype(BF16)
    far = lax.ppermute(partial, "dp", [(d, d ^ 2) for d in range(4)])
    grad_query, grad_key, grad_value, grad_filter = call(
        mix_kernel,
        (wide, wide, wide, shape(quarter.shape, F32)),
        "vvvvvvv hhhh",
        [pltpu.VMEM((3, *wide.shape), BF16), pltpu.VMEM(quarter.shape, F32), sems((CHUNKS + 1, 3))],
        flops=1 << 20,
        nbytes=4 << 20,
    )(returned, near, far, own, keys, values, cotan)
    return (grad_query[None], grad_key[None], grad_value[None], grad_filter)


def solution(mesh):
    tokens = P("dp", "seq", None)
    return jax.shard_map(
        on_device,
        mesh=mesh,
        in_specs=(tokens, tokens, tokens, tokens, P("seq", None)),
        out_specs=(tokens, tokens, tokens, P("seq", "dp")),
        check_vma=False,
    )
```

time: 63 us -> 57.8 us (0.917)
  Pallas kernels: 19 us -> 13.8 us
  waiting for transfers between devices: 21 us -> 23 us
  other arithmetic: 1.03 us -> 0.03 us
  local copies, waits for them, and re-layouts: 0.65 us -> 0 us
    pallas_call x5, Pallas kernels: 19 us -> 13.8 us  [run(): pl.pallas_call(kernel, out_shape=tuple((spaces[p](x.shape, x.dtype) for x...]
    all_to_all x2, waiting for transfers between devices: 10.9 us -> 12.4 us  [swap(): return lax.all_to_all(array, 'seq', split_axis=0, concat_axis=0, tiled=True)]
    convert_element_type x1, other arithmetic: 1.03 us -> 0.03 us  [on_device(): partial = (own[1].astype(F32) + near[1].astype(F32)).astype(BF16)]
    ppermute x1, waiting for transfers between devices: 8.7 us -> 9.43 us  [on_device(): far = lax.ppermute(partial, 'dp', [(d, d ^ 2) for d in range(4)])]
    unnamed x4 -> x0, local copies, waits for them, and re-layouts: 0.65 us -> none
  transfers between devices with their start and end apart: 4 -> 4, of which waited for: 3 -> 3; matrix products, arithmetic and copies ran while one was open for 2% -> 0% of each run, Pallas kernels for 11% -> 9%
where the time goes in v2:
time: 57.8 us; the launch traced here: 57.4 us
  waiting for transfers between devices  23 us (40%)
  starting transfers between devices  19.9 us (34%)
  Pallas kernels  13.8 us (24%)
  between operations  0.69 us (1%)
    all_to_all x2, starting transfers between devices, swap(): return lax.all_to_all(array, 'seq', split_axis=0, concat_axis=0, tiled=True)  15.7 us
    pallas_call x5, Pallas kernels, run(): pl.pallas_call(kernel, out_shape=tuple((spaces[p](x.shape, x.dtype) for x...  13.8 us
    all_to_all x2, waiting for transfers between devices, swap(): return lax.all_to_all(array, 'seq', split_axis=0, concat_axis=0, tiled=True)  12.4 us
    ppermute x1, waiting for transfers between devices, on_device(): far = lax.ppermute(partial, 'dp', [(d, d ^ 2) for d in range(4)])  9.43 us
    ppermute x1, starting transfers between devices, on_device(): far = lax.ppermute(partial, 'dp', [(d, d ^ 2) for d in range(4)])  2.7 us
    ppermute x1, starting transfers between devices, on_device(): near = lax.ppermute(sent_near, 'dp', [(d, d ^ 1) for d in range(4)])  1.53 us
    ppermute x1, waiting for transfers between devices, on_device(): near = lax.ppermute(sent_near, 'dp', [(d, d ^ 1) for d in range(4)])  1.16 us
  transfers between devices with their start and end apart: 4, of which 3 were waited for; matrix products, arithmetic and copies ran while one was open for 0% of the time, Pallas kernels for 9%

profile of v2, /device:TPU:1, one launch (start us, length us, event | category | flops | bytes accessed | tf_op | source)
XLA Modules:
  0.0 57.4 jit_solution(17428266576749838292)
XLA Ops:
  0.6 2.6 %shard_map.129 = bf16[32,128,128]{2,1,0:T(8,128)(2,1)} custom-call(bf16[128,2048]{1,0:T(8,128)(2,1)} %bitcast.16, bf16[128,2048]{1,0:T(8,128)(2,1)} %bitcast.10, bf16[128,2048]{1,0:T(8,128)(2,1)} %bitcast.12, bf16[128,2048]{1,0:T(8,128)(2,1)} %bitcast.14), custom_call_target="tpu_custom_call" | custom-call | flops 1048576 | bytes 3145728 | tf_op jit(solution)/shard_map/pallas_call | solution.py:272
  3.3 9.7 %all-to-all-start = ((bf16[32,128,128]{2,1,0:T(8,128)(2,1)}), bf16[32,128,128]{2,1,0:T(8,128)(2,1)S(1)}, u32[]{:S(2)}, u32[]{:S(2)}) async-start(bf16[32,128,128]{2,1,0:T(8,128)(2,1)} %shard_map.129), calls=%async_computation | async-start | bytes 2097152 | tf_op jit(solution)/shard_map/all_to_all | solution.py:286
  13.0 2.3 %shard_map.130 = (bf16[4,512,256]{2,1,0:T(8,128)(2,1)S(1)}, f32[2,32,128]{2,1,0:T(8,128)S(1)}, bf16[512,256]{1,0:T(8,128)(2,1)S(1)}, bf16[256,256]{1,0:T(8,128)(...) custom-call(f32[64,4096]{1,0:T(8,128)} %taps_hbm.1, f32[2,32,128]{2,1,0:T(8,128)} %constant.16.clone.twist_hbm, ...), custom_call_target="tpu_custom_call" | custom-call | flops 536870912 | bytes 3145728 | tf_op jit(solution)/shard_map/pallas_call | solution.py:272
  15.4 12.4 %all-to-all-done.data = bf16[32,128,128]{2,1,0:T(8,128)(2,1)S(1)} async-done(((bf16[32,128,128]{2,1,0:T(8,128)(2,1)}), bf16[32,128,128]{2,1,0:T(8,128)(2,1)S(1)}, u32[]{:S(2)}, u32[]{:S(2)}) %all-to-all-start) | async-done | bytes 1048608 | tf_op jit(solution)/shard_map/all_to_all | solution.py:286
  27.7 4.3 %shard_map.131 = (bf16[32,128,128]{2,1,0:T(8,128)(2,1)}, bf16[4,512,256]{2,1,0:T(8,128)(2,1)}) custom-call(bf16[32,128,128]{2,1,0:T(8,128)(2,1)S(1)} %all-to-all-done.data, bf16[4,512,256]{2,1,0:T(8,128)(2,1)S(1)} %get-tuple-element.21.filt, f32[2,32,128]{2,1,0:T(8,128)S(1)} %get-tuple-element.22.twist, bf16[512,256]{1,0:T(8,128)(2,1)S(1)} %get-tuple-element.23.first, ...), custom_call_target="tpu_custom_call" | custom-call | flops 2147483648 | bytes 5242880 | tf_op jit(solution)/shard_map/pallas_call | solution.py:272
  32.1 6.0 %all-to-all-start.1 = ((bf16[32,128,128]{2,1,0:T(8,128)(2,1)}), bf16[32,128,128]{2,1,0:T(8,128)(2,1)S(1)}, u32[]{:S(2)}, u32[]{:S(2)}) async-start(bf16[32,128,128]{2,1,0:T(8,128)(2,1)} %get-tuple-element.27), calls=%async_computation.1 | async-start | bytes 2097152 | tf_op jit(solution)/shard_map/all_to_all | solution.py:286
  38.0 2.9 %shard_map.132 = (bf16[2,64,1024]{2,1,0:T(8,128)(2,1)S(1)}, bf16[2,64,1024]{2,1,0:T(8,128)(2,1)S(1)}, bf16[128,2048]{1,0:T(8,128)(2,1)S(1)}, bf16[128,2048]{1,0:T(8,128)(2,1)S(1)}, bf16[128,2048]{1,0:T(8,128)(2,1)S(1)}) custom-call(s32[1]{0:T(128)} %bitcast.4.place_ref, bf16[4,512,256]{2,1,0:T(8,128)(2,1)} %get-tuple-element.28.cross_hbm, ...), custom_call_target="tpu_custom_call" | custom-call | flops 536870912 | bytes 3145728 | tf_op jit(solution)/shard_map/pallas_call | solution.py:272
  41.0 1.5 %collective-permute-start = (bf16[2,64,1024]{2,1,0:T(8,128)(2,1)S(1)}, bf16[2,64,1024]{2,1,0:T(8,128)(2,1)S(1)}, u32[]{:S(2)}, u32[]{:S(2)}) collective-permute-start(bf16[2,64,1024]{2,1,0:T(8,128)(2,1)S(1)} %get-tuple-element.29), channel_id=1, source_target_pairs={{0,32},{32,0},{64,96},{96,64},{1,33},{33,1},{65,97},{97,65},{2,34}... | collective-permute-start | bytes 786440 | tf_op jit(solution)/shard_map/ppermute | solution.py:339
  42.5 1.2 %collective-permute-done.near = bf16[2,64,1024]{2,1,0:T(8,128)(2,1)S(1)} collective-permute-done((bf16[2,64,1024]{2,1,0:T(8,128)(2,1)S(1)}, bf16[2,64,1024]{2,1,0:T(8,128)(2,1)S(1)}, u32[]{:S(2)}, u32[]{:S(2)}) %collective-permute-start) | collective-permute-done | bytes 262176 | tf_op jit(solution)/shard_map/ppermute | solution.py:339
  43.7 2.7 %collective-permute-start.1 = (bf16[64,1024]{1,0:T(8,128)(2,1)S(1)}, bf16[64,1024]{1,0:T(8,128)(2,1)S(1)}, u32[]{:S(2)}, u32[]{:S(2)}) collective-permute-start(bf16[64,1024]{1,0:T(8,128)(2,1)S(1)} %fusion), channel_id=1, source_target_pairs={{0,64},{32,96},{64,0},{96,32},{1,65},{33,97},{65,1},{97,33},{2,66}... | collective-permute-start | bytes 393224 | tf_op jit(solution)/shard_map/ppermute | solution.py:341
  46.4 9.4 %collective-permute-done.1.far = bf16[64,1024]{1,0:T(8,128)(2,1)S(1)} collective-permute-done((bf16[64,1024]{1,0:T(8,128)(2,1)S(1)}, bf16[64,1024]{1,0:T(8,128)(2,1)S(1)}, u32[]{:S(2)}, u32[]{:S(2)}) %collective-permute-start.1) | collective-permute-done | bytes 131104 | tf_op jit(solution)/shard_map/ppermute | solution.py:341
  55.8 0.0 all-to-all-done.1.data
  55.8 1.6 %shard_map.133 = (bf16[128,2048]{1,0:T(8,128)(2,1)}, bf16[128,2048]{1,0:T(8,128)(2,1)}, bf16[128,2048]{1,0:T(8,128)(2,1)}, f32[64,1024]{1,0:T(8,128)}) custom-call(bf16[32,128,128]{2,1,0:T(8,128)(2,1)S(1)} %all-to-all-done.1.data, bf16[2,64,1024]{2,1,0:T(8,128)(2,1)S(1)} %collective-permute-done.near, bf16[64,1024]{1,0:T(8,128)(2,1)S(1)} %collective-permute-done.1.far, ...), custom_call_target="tpu_custom_call" | custom-call | flops 1048576 | bytes 4194304 | tf_op jit(solution)/shard_map/pallas_call | solution.py:272
  (1 shorter events, 0.0 us)
Async XLA Ops:
  3.3 24.5 %all-to-all-start = ((bf16[32,128,128]{2,1,0:T(8,128)(2,1)}), bf16[32,128,128]{2,1,0:T(8,128)(2,1)S(1)}, u32[]{:S(2)}, u32[]{:S(2)}) async-start(bf16[32,128,128]{2,1,0:T(8,128)(2,1)} %shard_map.129), calls=%async_computation | async-start | bytes 2097152 | tf_op jit(solution)/shard_map/all_to_all | solution.py:286
  32.1 23.8 %all-to-all-start.1 = ((bf16[32,128,128]{2,1,0:T(8,128)(2,1)}), bf16[32,128,128]{2,1,0:T(8,128)(2,1)S(1)}, u32[]{:S(2)}, u32[]{:S(2)}) async-start(bf16[32,128,128]{2,1,0:T(8,128)(2,1)} %get-tuple-element.27), calls=%async_computation.1 | async-start | bytes 2097152 | tf_op jit(solution)/shard_map/all_to_all | solution.py:286
  41.0 2.7 %collective-permute-start = (bf16[2,64,1024]{2,1,0:T(8,128)(2,1)S(1)}, bf16[2,64,1024]{2,1,0:T(8,128)(2,1)S(1)}, u32[]{:S(2)}, u32[]{:S(2)}) collective-permute-start(bf16[2,64,1024]{2,1,0:T(8,128)(2,1)S(1)} %get-tuple-element.29), channel_id=1, source_target_pairs={{0,32},{32,0},{64,96},{96,64},{1,33},{33,1},{65,97},{97,65},{2,34}... | collective-permute-start | bytes 786440 | tf_op jit(solution)/shard_map/ppermute | solution.py:339
  43.7 12.1 %collective-permute-start.1 = (bf16[64,1024]{1,0:T(8,128)(2,1)S(1)}, bf16[64,1024]{1,0:T(8,128)(2,1)S(1)}, u32[]{:S(2)}, u32[]{:S(2)}) collective-permute-start(bf16[64,1024]{1,0:T(8,128)(2,1)S(1)} %fusion), channel_id=1, source_target_pairs={{0,64},{32,96},{64,0},{96,32},{1,65},{33,97},{65,1},{97,33},{2,66}... | collective-permute-start | bytes 393224 | tf_op jit(solution)/shard_map/ppermute | solution.py:341

commit v3 on v2

--- a/solution.py
+++ b/solution.py
@@ -20,6 +20,7 @@
 F32 = jnp.float32
 BF16 = jnp.bfloat16
 CHUNKS = 4
+GATE_BLOCKS = (10, 6)
 STEPS = OWN // PAIR
 VMEM_LIMIT = 24 * 1024 * 1024
 
@@ -123,17 +124,15 @@
 
 def gate_kernel(query_hbm, key_hbm, value_hbm, cotan_hbm, out_hbm, held, sent, in_sems, out_sems):
     sources = (key_hbm, value_hbm, query_hbm, cotan_hbm)
-    span = held.shape[2] // CHUNKS
-    pairs = []
-    for chunk in range(CHUNKS):
-        lanes = pl.ds(chunk * span, span)
+    pairs, starts = [], [sum(GATE_BLOCKS[:chunk]) for chunk in range(len(GATE_BLOCKS) + 1)]
+    for low, high in zip(starts[:-1], starts[1:]):
+        lanes = pl.ds(low * COLS, (high - low) * COLS)
         pairs += [(source.at[:, lanes], held.at[place, :, lanes]) for place, source in enumerate(sources)]
     arriving = copies_of(pairs, in_sems)
     leaving = []
-    for chunk in range(CHUNKS):
+    for chunk, (low, high) in enumerate(zip(starts[:-1], starts[1:])):
         wait_all(arriving[4 * chunk : 4 * chunk + 4])
-        first_block, last_block = chunk * span // COLS, (chunk + 1) * span // COLS
-        for block in range(first_block, last_block):
+        for block in range(low, high):
             lanes = pl.ds(block * COLS, COLS)
             for part in range(2):
                 left, right = held[2 * part, :, lanes].astype(F32), held[2 * part + 1, :, lanes].astype(F32)
@@ -141,7 +140,7 @@
                 rows = slice(part * OWN, (part + 1) * OWN)
                 sent[2 * block, rows] = turned[:OWN]
                 sent[2 * block + 1, rows] = turned[OWN:]
-        dests = pl.ds(2 * first_block, 2 * (last_block - first_block))
+        dests = pl.ds(2 * low, 2 * (high - low))
         copy = pltpu.make_async_copy(sent.at[dests], out_hbm.at[dests], out_sems.at[chunk])
         copy.start()
         leaving.append(copy)
@@ -181,17 +180,24 @@
 
 def conv_kernel(data, filt, twist, first, ahead, last, back, out_hbm, cross_hbm, out, cross, out_sems):
     leaving = []
-    for step in range(STEPS):
+    prods = []
+    for many in range(0, STEPS, 2):
         blocks = []
-        for part in range(2):
-            rows = slice(part * OWN + step * PAIR, part * OWN + (step + 1) * PAIR)
-            blocks.append(split_rows(data[:, rows, :]))
+        for step in range(many, many + 2):
+            for part in range(2):
+                rows = slice(part * OWN + step * PAIR, part * OWN + (step + 1) * PAIR)
+                blocks.append(split_rows(data[:, rows, :]))
         specs = spectra(blocks, twist, first, ahead)
-        gated, grads, turn = specs[: 2 * BLOCK], specs[2 * BLOCK :], filt[step]
-        cross[step] = product(gated, grads, True).astype(BF16)
-        leaving += copies_of([(cross.at[step], cross_hbm.at[step])], out_sems.at[step, 2:])
-        prods = jnp.concatenate([product(turn, gated, False), product(turn, grads, True)], axis=0)
-        for part, block in enumerate(unturned(prods, twist, back)):
+        for step in range(many, many + 2):
+            low = (step - many) * 4 * BLOCK
+            gated, grads, turn = specs[low : low + 2 * BLOCK], specs[low + 2 * BLOCK : low + 4 * BLOCK], filt[step]
+            cross[step] = product(gated, grads, True).astype(BF16)
+            leaving += copies_of([(cross.at[step], cross_hbm.at[step])], out_sems.at[step, 2:])
+            prods += [product(turn, gated, False).astype(BF16), product(turn, grads, True).astype(BF16)]
+    for many in range(0, STEPS, 1):
+        blocks = unturned(jnp.concatenate(prods[2 * many : 2 * (many + 1)], axis=0), twist, back)
+        for place, block in enumerate(blocks):
+            step, part = many + place // 2, place % 2
             rows = slice(part * OWN + step * PAIR, part * OWN + (step + 1) * PAIR)
             out[:, rows, :] = lags_of(block, last).astype(BF16)
             leaving += copies_of([(out.at[:, rows, :], out_hbm.at[:, rows, :])], out_sems.at[step, part:])
@@ -304,7 +310,7 @@
         gate_kernel,
         (cube,),
         "hhhh h",
-        [pltpu.VMEM((4, *query.shape), BF16), *room(cube), sems((4 * CHUNKS,)), sems((CHUNKS,))],
+        [pltpu.VMEM((4, *query.shape), BF16), *room(cube), sems((4 * len(GATE_BLOCKS),)), sems((len(GATE_BLOCKS),))],
         flops=1 << 20,
         nbytes=3 << 20,
     )(query, keys, values, cotan)

time: 57.8 us -> 57.3 us (level)
  no operation moved by 1% of the time
where the time goes in v3:
time: 57.3 us; the launch traced here: 56.9 us
  waiting for transfers between devices  22.9 us (40%)
  starting transfers between devices  19.9 us (35%)
  Pallas kernels  13.4 us (23%)
  between operations  0.69 us (1%)
    all_to_all x2, starting transfers between devices, swap(): return lax.all_to_all(array, 'seq', split_axis=0, concat_axis=0, tiled=True)  15.7 us
    pallas_call x5, Pallas kernels, run(): pl.pallas_call(kernel, out_shape=tuple((spaces[p](x.shape, x.dtype) for x...  13.4 us
    all_to_all x2, waiting for transfers between devices, swap(): return lax.all_to_all(array, 'seq', split_axis=0, concat_axis=0, tiled=True)  12.4 us
    ppermute x1, waiting for transfers between devices, on_device(): far = lax.ppermute(partial, 'dp', [(d, d ^ 2) for d in range(4)])  9.42 us
    ppermute x1, starting transfers between devices, on_device(): far = lax.ppermute(partial, 'dp', [(d, d ^ 2) for d in range(4)])  2.7 us
    ppermute x1, starting transfers between devices, on_device(): near = lax.ppermute(sent_near, 'dp', [(d, d ^ 1) for d in range(4)])  1.53 us
    ppermute x1, waiting for transfers between devices, on_device(): near = lax.ppermute(sent_near, 'dp', [(d, d ^ 1) for d in range(4)])  1.16 us
  transfers between devices with their start and end apart: 4, of which 3 were waited for; matrix products, arithmetic and copies ran while one was open for 0% of the time, Pallas kernels for 9%

profile of v3, /device:TPU:1, one launch (start us, length us, event | category | flops | bytes accessed | tf_op | source)
XLA Modules:
  0.0 56.9 jit_solution(12049619618250533149)
XLA Ops:
  0.6 2.6 %shard_map.129 = bf16[32,128,128]{2,1,0:T(8,128)(2,1)} custom-call(bf16[128,2048]{1,0:T(8,128)(2,1)} %bitcast.16, bf16[128,2048]{1,0:T(8,128)(2,1)} %bitcast.10, bf16[128,2048]{1,0:T(8,128)(2,1)} %bitcast.12, bf16[128,2048]{1,0:T(8,128)(2,1)} %bitcast.14), custom_call_target="tpu_custom_call" | custom-call | flops 1048576 | bytes 3145728 | tf_op jit(solution)/shard_map/pallas_call | solution.py:278
  3.2 9.7 %all-to-all-start = ((bf16[32,128,128]{2,1,0:T(8,128)(2,1)}), bf16[32,128,128]{2,1,0:T(8,128)(2,1)S(1)}, u32[]{:S(2)}, u32[]{:S(2)}) async-start(bf16[32,128,128]{2,1,0:T(8,128)(2,1)} %shard_map.129), calls=%async_computation | async-start | bytes 2097152 | tf_op jit(solution)/shard_map/all_to_all | solution.py:292
  13.0 2.3 %shard_map.130 = (bf16[4,512,256]{2,1,0:T(8,128)(2,1)S(1)}, f32[2,32,128]{2,1,0:T(8,128)S(1)}, bf16[512,256]{1,0:T(8,128)(2,1)S(1)}, bf16[256,256]{1,0:T(8,128)(...) custom-call(f32[64,4096]{1,0:T(8,128)} %taps_hbm.1, f32[2,32,128]{2,1,0:T(8,128)} %constant.16.clone.twist_hbm, ...), custom_call_target="tpu_custom_call" | custom-call | flops 536870912 | bytes 3145728 | tf_op jit(solution)/shard_map/pallas_call | solution.py:278
  15.3 12.4 %all-to-all-done.data = bf16[32,128,128]{2,1,0:T(8,128)(2,1)S(1)} async-done(((bf16[32,128,128]{2,1,0:T(8,128)(2,1)}), bf16[32,128,128]{2,1,0:T(8,128)(2,1)S(1)}, u32[]{:S(2)}, u32[]{:S(2)}) %all-to-all-start) | async-done | bytes 1048608 | tf_op jit(solution)/shard_map/all_to_all | solution.py:292
  27.7 3.9 %shard_map.131 = (bf16[32,128,128]{2,1,0:T(8,128)(2,1)}, bf16[4,512,256]{2,1,0:T(8,128)(2,1)}) custom-call(bf16[32,128,128]{2,1,0:T(8,128)(2,1)S(1)} %all-to-all-done.data, bf16[4,512,256]{2,1,0:T(8,128)(2,1)S(1)} %get-tuple-element.21.filt, f32[2,32,128]{2,1,0:T(8,128)S(1)} %get-tuple-element.22.twist, bf16[512,256]{1,0:T(8,128)(2,1)S(1)} %get-tuple-element.23.first, ...), custom_call_target="tpu_custom_call" | custom-call | flops 2147483648 | bytes 5242880 | tf_op jit(solution)/shard_map/pallas_call | solution.py:278
  31.6 5.9 %all-to-all-start.1 = ((bf16[32,128,128]{2,1,0:T(8,128)(2,1)}), bf16[32,128,128]{2,1,0:T(8,128)(2,1)S(1)}, u32[]{:S(2)}, u32[]{:S(2)}) async-start(bf16[32,128,128]{2,1,0:T(8,128)(2,1)} %get-tuple-element.27), calls=%async_computation.1 | async-start | bytes 2097152 | tf_op jit(solution)/shard_map/all_to_all | solution.py:292
  37.6 2.9 %shard_map.132 = (bf16[2,64,1024]{2,1,0:T(8,128)(2,1)S(1)}, bf16[2,64,1024]{2,1,0:T(8,128)(2,1)S(1)}, bf16[128,2048]{1,0:T(8,128)(2,1)S(1)}, bf16[128,2048]{1,0:T(8,128)(2,1)S(1)}, bf16[128,2048]{1,0:T(8,128)(2,1)S(1)}) custom-call(s32[1]{0:T(128)} %bitcast.4.place_ref, bf16[4,512,256]{2,1,0:T(8,128)(2,1)} %get-tuple-element.28.cross_hbm, ...), custom_call_target="tpu_custom_call" | custom-call | flops 536870912 | bytes 3145728 | tf_op jit(solution)/shard_map/pallas_call | solution.py:278
  40.5 1.5 %collective-permute-start = (bf16[2,64,1024]{2,1,0:T(8,128)(2,1)S(1)}, bf16[2,64,1024]{2,1,0:T(8,128)(2,1)S(1)}, u32[]{:S(2)}, u32[]{:S(2)}) collective-permute-start(bf16[2,64,1024]{2,1,0:T(8,128)(2,1)S(1)} %get-tuple-element.29), channel_id=1, source_target_pairs={{0,32},{32,0},{64,96},{96,64},{1,33},{33,1},{65,97},{97,65},{2,34}... | collective-permute-start | bytes 786440 | tf_op jit(solution)/shard_map/ppermute | solution.py:345
  42.0 1.2 %collective-permute-done.near = bf16[2,64,1024]{2,1,0:T(8,128)(2,1)S(1)} collective-permute-done((bf16[2,64,1024]{2,1,0:T(8,128)(2,1)S(1)}, bf16[2,64,1024]{2,1,0:T(8,128)(2,1)S(1)}, u32[]{:S(2)}, u32[]{:S(2)}) %collective-permute-start) | collective-permute-done | bytes 262176 | tf_op jit(solution)/shard_map/ppermute | solution.py:345
  43.2 2.7 %collective-permute-start.1 = (bf16[64,1024]{1,0:T(8,128)(2,1)S(1)}, bf16[64,1024]{1,0:T(8,128)(2,1)S(1)}, u32[]{:S(2)}, u32[]{:S(2)}) collective-permute-start(bf16[64,1024]{1,0:T(8,128)(2,1)S(1)} %fusion), channel_id=1, source_target_pairs={{0,64},{32,96},{64,0},{96,32},{1,65},{33,97},{65,1},{97,33},{2,66}... | collective-permute-start | bytes 393224 | tf_op jit(solution)/shard_map/ppermute | solution.py:347
  45.9 9.4 %collective-permute-done.1.far = bf16[64,1024]{1,0:T(8,128)(2,1)S(1)} collective-permute-done((bf16[64,1024]{1,0:T(8,128)(2,1)S(1)}, bf16[64,1024]{1,0:T(8,128)(2,1)S(1)}, u32[]{:S(2)}, u32[]{:S(2)}) %collective-permute-start.1) | collective-permute-done | bytes 131104 | tf_op jit(solution)/shard_map/ppermute | solution.py:347
  55.3 0.0 all-to-all-done.1.data
  55.3 1.6 %shard_map.133 = (bf16[128,2048]{1,0:T(8,128)(2,1)}, bf16[128,2048]{1,0:T(8,128)(2,1)}, bf16[128,2048]{1,0:T(8,128)(2,1)}, f32[64,1024]{1,0:T(8,128)}) custom-call(bf16[32,128,128]{2,1,0:T(8,128)(2,1)S(1)} %all-to-all-done.1.data, bf16[2,64,1024]{2,1,0:T(8,128)(2,1)S(1)} %collective-permute-done.near, bf16[64,1024]{1,0:T(8,128)(2,1)S(1)} %collective-permute-done.1.far, ...), custom_call_target="tpu_custom_call" | custom-call | flops 1048576 | bytes 4194304 | tf_op jit(solution)/shard_map/pallas_call | solution.py:278
  (1 shorter events, 0.0 us)
Async XLA Ops:
  3.2 24.5 %all-to-all-start = ((bf16[32,128,128]{2,1,0:T(8,128)(2,1)}), bf16[32,128,128]{2,1,0:T(8,128)(2,1)S(1)}, u32[]{:S(2)}, u32[]{:S(2)}) async-start(bf16[32,128,128]{2,1,0:T(8,128)(2,1)} %shard_map.129), calls=%async_computation | async-start | bytes 2097152 | tf_op jit(solution)/shard_map/all_to_all | solution.py:292
  31.6 23.8 %all-to-all-start.1 = ((bf16[32,128,128]{2,1,0:T(8,128)(2,1)}), bf16[32,128,128]{2,1,0:T(8,128)(2,1)S(1)}, u32[]{:S(2)}, u32[]{:S(2)}) async-start(bf16[32,128,128]{2,1,0:T(8,128)(2,1)} %get-tuple-element.27), calls=%async_computation.1 | async-start | bytes 2097152 | tf_op jit(solution)/shard_map/all_to_all | solution.py:292
  40.5 2.7 %collective-permute-start = (bf16[2,64,1024]{2,1,0:T(8,128)(2,1)S(1)}, bf16[2,64,1024]{2,1,0:T(8,128)(2,1)S(1)}, u32[]{:S(2)}, u32[]{:S(2)}) collective-permute-start(bf16[2,64,1024]{2,1,0:T(8,128)(2,1)S(1)} %get-tuple-element.29), channel_id=1, source_target_pairs={{0,32},{32,0},{64,96},{96,64},{1,33},{33,1},{65,97},{97,65},{2,34}... | collective-permute-start | bytes 786440 | tf_op jit(solution)/shard_map/ppermute | solution.py:345
  43.2 12.1 %collective-permute-start.1 = (bf16[64,1024]{1,0:T(8,128)(2,1)S(1)}, bf16[64,1024]{1,0:T(8,128)(2,1)S(1)}, u32[]{:S(2)}, u32[]{:S(2)}) collective-permute-start(bf16[64,1024]{1,0:T(8,128)(2,1)S(1)} %fusion), channel_id=1, source_target_pairs={{0,64},{32,96},{64,0},{96,32},{1,65},{33,97},{65,1},{97,33},{2,66}... | collective-permute-start | bytes 393224 | tf_op jit(solution)/shard_map/ppermute | solution.py:347

commit v4 on v3

--- a/solution.py
+++ b/solution.py
@@ -21,6 +21,7 @@
 BF16 = jnp.bfloat16
 CHUNKS = 4
 GATE_BLOCKS = (10, 6)
+LATE_CHUNKS = 4
 STEPS = OWN // PAIR
 VMEM_LIMIT = 24 * 1024 * 1024
 
@@ -122,29 +123,49 @@
         copy.wait()
 
 
-def gate_kernel(query_hbm, key_hbm, value_hbm, cotan_hbm, out_hbm, held, sent, in_sems, out_sems):
+def gate_blocks(held, sent, low, count):
+    for place in range(count):
+        block = low + place
+        lanes = pl.ds(block * COLS if isinstance(block, int) else pl.multiple_of(block * COLS, COLS), COLS)
+        for part in range(2):
+            left, right = held[2 * part, :, lanes].astype(F32), held[2 * part + 1, :, lanes].astype(F32)
+            turned = (left * right).T.astype(BF16)
+            rows = slice(part * OWN, (part + 1) * OWN)
+            sent[2 * block, rows] = turned[:OWN]
+            sent[2 * block + 1, rows] = turned[OWN:]
+
+
+def gate_kernel(place_ref, query_hbm, key_hbm, value_hbm, cotan_hbm, out_hbm, held, sent, in_sems, out_sems):
     sources = (key_hbm, value_hbm, query_hbm, cotan_hbm)
-    pairs, starts = [], [sum(GATE_BLOCKS[:chunk]) for chunk in range(len(GATE_BLOCKS) + 1)]
-    for low, high in zip(starts[:-1], starts[1:]):
-        lanes = pl.ds(low * COLS, (high - low) * COLS)
-        pairs += [(source.at[:, lanes], held.at[place, :, lanes]) for place, source in enumerate(sources)]
-    arriving = copies_of(pairs, in_sems)
-    leaving = []
-    for chunk, (low, high) in enumerate(zip(starts[:-1], starts[1:])):
-        wait_all(arriving[4 * chunk : 4 * chunk + 4])
-        for block in range(low, high):
-            lanes = pl.ds(block * COLS, COLS)
-            for part in range(2):
-                left, right = held[2 * part, :, lanes].astype(F32), held[2 * part + 1, :, lanes].astype(F32)
-                turned = (left * right).T.astype(BF16)
-                rows = slice(part * OWN, (part + 1) * OWN)
-                sent[2 * block, rows] = turned[:OWN]
-                sent[2 * block + 1, rows] = turned[OWN:]
-        dests = pl.ds(2 * low, 2 * (high - low))
-        copy = pltpu.make_async_copy(sent.at[dests], out_hbm.at[dests], out_sems.at[chunk])
-        copy.start()
-        leaving.append(copy)
-    wait_all(leaving)
+    core = jnp.bitwise_and(place_ref[0], 1)
+
+    @pl.when(core == 1)
+    def _():
+        pairs, starts = [], [sum(GATE_BLOCKS[:chunk]) for chunk in range(len(GATE_BLOCKS) + 1)]
+        for low, high in zip(starts[:-1], starts[1:]):
+            lanes = pl.ds(low * COLS, (high - low) * COLS)
+            pairs += [(source.at[:, lanes], held.at[place, :, lanes]) for place, source in enumerate(sources)]
+        arriving = copies_of(pairs, in_sems)
+        leaving = []
+        for chunk, (low, high) in enumerate(zip(starts[:-1], starts[1:])):
+            wait_all(arriving[4 * chunk : 4 * chunk + 4])
+            gate_blocks(held, sent, low, high - low)
+            dests = pl.ds(2 * low, 2 * (high - low))
+            leaving += copies_of([(sent.at[dests], out_hbm.at[dests])], out_sems.at[chunk : chunk + 1])
+        wait_all(leaving)
+
+    @pl.when(core == 0)
+    def _():
+        count = held.shape[2] // COLS // LATE_CHUNKS
+
+        @pl.loop(0, LATE_CHUNKS)
+        def _(chunk):
+            lanes = pl.ds(pl.multiple_of(chunk * count * COLS, COLS), count * COLS)
+            pairs = [(source.at[:, lanes], held.at[place, :, lanes]) for place, source in enumerate(sources)]
+            wait_all(copies_of(pairs, in_sems))
+            gate_blocks(held, sent, chunk * count, count)
+            dests = pl.ds(2 * chunk * count, 2 * count)
+            wait_all(copies_of([(sent.at[dests], out_hbm.at[dests])], out_sems))
 
 
 def filter_kernel(
@@ -178,9 +199,9 @@
     wait_all(arriving[4:])
 
 
-def conv_kernel(data, filt, twist, first, ahead, last, back, out_hbm, cross_hbm, out, cross, out_sems):
+def conv_kernel(place_ref, data, filt, twist, first, ahead, last, back, out_hbm, own, near, out, terms, out_sems):
     leaving = []
-    prods = []
+    prods, cross = [], []
     for many in range(0, STEPS, 2):
         blocks = []
         for step in range(many, many + 2):
@@ -191,54 +212,31 @@
         for step in range(many, many + 2):
             low = (step - many) * 4 * BLOCK
             gated, grads, turn = specs[low : low + 2 * BLOCK], specs[low + 2 * BLOCK : low + 4 * BLOCK], filt[step]
-            cross[step] = product(gated, grads, True).astype(BF16)
-            leaving += copies_of([(cross.at[step], cross_hbm.at[step])], out_sems.at[step, 2:])
-            prods += [product(turn, gated, False).astype(BF16), product(turn, grads, True).astype(BF16)]
-    for many in range(0, STEPS, 1):
-        blocks = unturned(jnp.concatenate(prods[2 * many : 2 * (many + 1)], axis=0), twist, back)
-        for place, block in enumerate(blocks):
-            step, part = many + place // 2, place % 2
+            cross.append(product(gated, grads, True).astype(BF16))
+            prods.append(jnp.concatenate([product(turn, gated, False), product(turn, grads, True)], axis=0).astype(BF16))
+    for step in range(STEPS):
+        for part, block in enumerate(unturned(prods[step], twist, back)):
             rows = slice(part * OWN + step * PAIR, part * OWN + (step + 1) * PAIR)
             out[:, rows, :] = lags_of(block, last).astype(BF16)
             leaving += copies_of([(out.at[:, rows, :], out_hbm.at[:, rows, :])], out_sems.at[step, part:])
-    wait_all(leaving)
-
-
-def taps_kernel(
-    place_ref,
-    cross_hbm,
-    key_hbm,
-    value_hbm,
-    cotan_hbm,
-    twist,
-    last,
-    back,
-    own,
-    near,
-    keys,
-    values,
-    cotan,
-    cross,
-    lags_ref,
-    sems,
-    out_sems,
-):
-    pairs = [(cross_hbm, cross), (key_hbm, keys), (value_hbm, values), (cotan_hbm, cotan)]
-    arriving = copies_of(pairs, sems)
-    arriving[0].wait()
     per = ROWS // 4
     for step in range(STEPS):
-        lags = lags_of(unturned(cross[step], twist, back)[0], last).astype(BF16)
+        (block,) = unturned(cross[step], twist, back)
+        lags = lags_of(block, last).astype(BF16)
         rows = slice(step * PAIR, (step + 1) * PAIR)
         for p in range(ROWS):
-            lags_ref[p // per, rows, (p % per) * COLS : (p % per + 1) * COLS] = lags[p]
+            terms[p // per, rows, (p % per) * COLS : (p % per + 1) * COLS] = lags[p]
     place = place_ref[0]
-    pairs = []
     for shift in range(4):
         target = (own, near)[shift % 2]
-        pairs.append((lags_ref.at[jnp.bitwise_xor(place, shift)], target.at[shift // 2]))
-    wait_all(copies_of(pairs, out_sems))
-    wait_all(arriving[1:])
+        target[shift // 2] = terms[jnp.bitwise_xor(place, shift)]
+    wait_all(leaving)
+
+
+def bring_kernel(terms, key_hbm, value_hbm, cotan_hbm, own, keys, values, cotan, sems):
+    copies = copies_of([(key_hbm, keys), (value_hbm, values), (cotan_hbm, cotan)], sems)
+    own[...] = terms[0]
+    wait_all(copies)
 
 
 def mix_kernel(
@@ -247,7 +245,7 @@
     span = keys.shape[1] // CHUNKS
     factors = (cotan, values, keys)
     outs = (query_out, key_out, value_out)
-    whole = own[0].astype(F32) + near[0].astype(F32) + far[...].astype(F32)
+    whole = own[...].astype(F32) + near[0].astype(F32) + far[...].astype(F32)
     total[...] = whole * (1.0 / math.sqrt(4 * TOKENS))
     leaving = copies_of([(total, filter_out)], out_sems.at[CHUNKS])
     for chunk in range(CHUNKS):
@@ -306,14 +304,15 @@
     def room(*arrays):
         return [pltpu.VMEM(array.shape, array.dtype) for array in arrays]
 
+    place = lax.axis_index("dp").astype(jnp.int32).reshape(1)
     (sent,) = call(
         gate_kernel,
         (cube,),
-        "hhhh h",
+        "shhhh h",
         [pltpu.VMEM((4, *query.shape), BF16), *room(cube), sems((4 * len(GATE_BLOCKS),)), sems((len(GATE_BLOCKS),))],
         flops=1 << 20,
         nbytes=3 << 20,
-    )(query, keys, values, cotan)
+    )(place, query, keys, values, cotan)
     filt, twist, first, ahead, last, back = call(
         filter_kernel,
         (filt_spec, twist, first, ahead, last, back),
@@ -323,27 +322,26 @@
         nbytes=3 << 20,
     )(filter_taps, twist, first, ahead, last, back)
     data = swap(sent)
-    result, cross = call(
+    half = shape((2, *quarter.shape), BF16)
+    result, terms, sent_near = call(
         conv_kernel,
-        (cube, filt_spec),
-        "vvvvvvv hh",
-        [*room(cube, filt_spec), sems((STEPS, 3))],
+        (cube, half, half),
+        "svvvvvvv hvv",
+        [*room(cube), pltpu.VMEM((4, *quarter.shape), BF16), sems((STEPS, 2))],
         flops=2 * unit,
         nbytes=5 << 20,
-    )(data, filt, twist, first, ahead, last, back)
+    )(place, data, filt, twist, first, ahead, last, back)
+    near = lax.ppermute(sent_near, "dp", [(d, d ^ 1) for d in range(4)])
     returned = swap(result)
-    place = lax.axis_index("dp").astype(jnp.int32).reshape(1)
-    half = shape((2, *quarter.shape), BF16)
-    own, sent_near, keys, values, cotan = call(
-        taps_kernel,
-        (half, half, wide, wide, wide),
-        "shhhhvvv vvvvv",
-        [*room(filt_spec), pltpu.VMEM((4, *quarter.shape), BF16), sems((4,)), sems((4,))],
-        flops=unit // 2,
+    own, keys, values, cotan = call(
+        bring_kernel,
+        (quarter, wide, wide, wide),
+        "vhhh vvvv",
+        [sems((3,))],
+        flops=1 << 20,
         nbytes=3 << 20,
-    )(place, cross, keys, values, cotan, twist, last, back)
-    near = lax.ppermute(sent_near, "dp", [(d, d ^ 1) for d in range(4)])
-    partial = (own[1].astype(F32) + near[1].astype(F32)).astype(BF16)
+    )(terms, keys, values, cotan)
+    partial = (terms[1].astype(F32) + near[1].astype(F32)).astype(BF16)
     far = lax.ppermute(partial, "dp", [(d, d ^ 2) for d in range(4)])
     grad_query, grad_key, grad_value, grad_filter = call(
         mix_kernel,

time: 57.3 us -> 54.2 us (0.946)
  waiting for transfers between devices: 22.9 us -> 16.5 us
  starting transfers between devices: 19.9 us -> 24.4 us
  Pallas kernels: 13.4 us -> 11.9 us
    ppermute x1, starting transfers between devices: 1.53 us -> 7.98 us  [on_device(): near = lax.ppermute(sent_near, 'dp', [(d, d ^ 1) for d in range(4)])]
    ppermute x1, waiting for transfers between devices: 9.42 us -> 6.14 us  [on_device(): far = lax.ppermute(partial, 'dp', [(d, d ^ 2) for d in range(4)])]
    all_to_all x2, waiting for transfers between devices: 12.4 us -> 9.16 us  [swap(): return lax.all_to_all(array, 'seq', split_axis=0, concat_axis=0, tiled=True)]
    all_to_all x2, starting transfers between devices: 15.7 us -> 13.8 us  [swap(): return lax.all_to_all(array, 'seq', split_axis=0, concat_axis=0, tiled=True)]
    pallas_call x5, Pallas kernels: 13.4 us -> 11.9 us  [run(): pl.pallas_call(kernel, out_shape=tuple((spaces[p](x.shape, x.dtype) for x...]
  transfers between devices with their start and end apart: 4 -> 4, of which waited for: 3 -> 3; matrix products, arithmetic and copies ran while one was open for 0% -> 0% of each run, Pallas kernels for 9% -> 7%
where the time goes in v4:
time: 54.2 us; the launch traced here: 53.5 us
  starting transfers between devices  24.4 us (45%)
  waiting for transfers between devices  16.5 us (30%)
  Pallas kernels  11.9 us (22%)
  between operations  0.69 us (1%)
    all_to_all x2, starting transfers between devices, swap(): return lax.all_to_all(array, 'seq', split_axis=0, concat_axis=0, tiled=True)  13.8 us
    pallas_call x5, Pallas kernels, run(): pl.pallas_call(kernel, out_shape=tuple((spaces[p](x.shape, x.dtype) for x...  11.9 us
    all_to_all x2, waiting for transfers between devices, swap(): return lax.all_to_all(array, 'seq', split_axis=0, concat_axis=0, tiled=True)  9.16 us
    ppermute x1, starting transfers between devices, on_device(): near = lax.ppermute(sent_near, 'dp', [(d, d ^ 1) for d in range(4)])  7.98 us
    ppermute x1, waiting for transfers between devices, on_device(): far = lax.ppermute(partial, 'dp', [(d, d ^ 2) for d in range(4)])  6.14 us
    ppermute x1, starting transfers between devices, on_device(): far = lax.ppermute(partial, 'dp', [(d, d ^ 2) for d in range(4)])  2.7 us
    ppermute x1, waiting for transfers between devices, on_device(): near = lax.ppermute(sent_near, 'dp', [(d, d ^ 1) for d in range(4)])  1.16 us
  transfers between devices with their start and end apart: 4, of which 3 were waited for; matrix products, arithmetic and copies ran while one was open for 0% of the time, Pallas kernels for 7%

profile of v4, /device:TPU:1, one launch (start us, length us, event | category | flops | bytes accessed | tf_op | source)
XLA Modules:
  0.0 53.5 jit_solution(6954994799946183077)
XLA Ops:
  0.6 2.6 %shard_map.129 = bf16[32,128,128]{2,1,0:T(8,128)(2,1)} custom-call(s32[1]{0:T(128)} %bitcast.place_ref, bf16[128,2048]{1,0:T(8,128)(2,1)} %bitcast.16, bf16[128,2048]{1,0:T(8,128)(2,1)} %bitcast.10, bf16[128,2048]{1,0:T(8,128)(2,1)} %bitcast.12, bf16[128,2048]{1,0:T(8,128)(2,1)} %bitcast.14), custom_call_target="tpu_custom_call" | custom-call | flops 1048576 | bytes 3145728 | tf_op jit(solution)/shard_map/pallas_call | solution.py:276
  3.2 9.7 %all-to-all-start = ((bf16[32,128,128]{2,1,0:T(8,128)(2,1)}), bf16[32,128,128]{2,1,0:T(8,128)(2,1)S(1)}, u32[]{:S(2)}, u32[]{:S(2)}) async-start(bf16[32,128,128]{2,1,0:T(8,128)(2,1)} %shard_map.129), calls=%async_computation | async-start | bytes 2097152 | tf_op jit(solution)/shard_map/all_to_all | solution.py:290
  13.0 2.3 %shard_map.130 = (bf16[4,512,256]{2,1,0:T(8,128)(2,1)S(1)}, f32[2,32,128]{2,1,0:T(8,128)S(1)}, bf16[512,256]{1,0:T(8,128)(2,1)S(1)}, bf16[256,256]{1,0:T(8,128)(...) custom-call(f32[64,4096]{1,0:T(8,128)} %taps_hbm.1, f32[2,32,128]{2,1,0:T(8,128)} %constant.16.clone.twist_hbm, ...), custom_call_target="tpu_custom_call" | custom-call | flops 536870912 | bytes 3145728 | tf_op jit(solution)/shard_map/pallas_call | solution.py:276
  15.3 9.2 %all-to-all-done.data = bf16[32,128,128]{2,1,0:T(8,128)(2,1)S(1)} async-done(((bf16[32,128,128]{2,1,0:T(8,128)(2,1)}), bf16[32,128,128]{2,1,0:T(8,128)(2,1)S(1)}, u32[]{:S(2)}, u32[]{:S(2)}) %all-to-all-start) | async-done | bytes 1048608 | tf_op jit(solution)/shard_map/all_to_all | solution.py:290
  24.5 4.0 %shard_map.131 = (bf16[32,128,128]{2,1,0:T(8,128)(2,1)}, bf16[2,64,1024]{2,1,0:T(8,128)(2,1)S(1)}, bf16[2,64,1024]{2,1,0:T(8,128)(2,1)S(1)}) custom-call(s32[1]{0:T(128)} %bitcast.place_ref, bf16[32,128,128]{2,1,0:T(8,128)(2,1)S(1)} %all-to-all-done.data, bf16[4,512,256]{2,1,0:T(8,128)(2,1)S(1)} %get-tuple-element.21.filt, ...), custom_call_target="tpu_custom_call" | custom-call | flops 2147483648 | bytes 5242880 | tf_op jit(solution)/shard_map/pallas_call | solution.py:276
  28.5 4.0 %all-to-all-start.1 = ((bf16[32,128,128]{2,1,0:T(8,128)(2,1)}), bf16[32,128,128]{2,1,0:T(8,128)(2,1)S(1)}, u32[]{:S(2)}, u32[]{:S(2)}) async-start(bf16[32,128,128]{2,1,0:T(8,128)(2,1)} %get-tuple-element.27), calls=%async_computation.1 | async-start | bytes 2097152 | tf_op jit(solution)/shard_map/all_to_all | solution.py:290
  32.5 8.0 %collective-permute-start = (bf16[2,64,1024]{2,1,0:T(8,128)(2,1)S(1)}, bf16[2,64,1024]{2,1,0:T(8,128)(2,1)S(1)}, u32[]{:S(2)}, u32[]{:S(2)}) collective-permute-start(bf16[2,64,1024]{2,1,0:T(8,128)(2,1)S(1)} %get-tuple-element.28), channel_id=1, source_target_pairs={{0,32},{32,0},{64,96},{96,64},{1,33},{33,1},{65,97},{97,65},{2,34}... | collective-permute-start | bytes 786440 | tf_op jit(solution)/shard_map/ppermute | solution.py:334
  40.5 1.2 %collective-permute-done.near = bf16[2,64,1024]{2,1,0:T(8,128)(2,1)S(1)} collective-permute-done((bf16[2,64,1024]{2,1,0:T(8,128)(2,1)S(1)}, bf16[2,64,1024]{2,1,0:T(8,128)(2,1)S(1)}, u32[]{:S(2)}, u32[]{:S(2)}) %collective-permute-start) | collective-permute-done | bytes 262176 | tf_op jit(solution)/shard_map/ppermute | solution.py:334
  41.7 2.7 %collective-permute-start.1 = (bf16[64,1024]{1,0:T(8,128)(2,1)S(1)}, bf16[64,1024]{1,0:T(8,128)(2,1)S(1)}, u32[]{:S(2)}, u32[]{:S(2)}) collective-permute-start(bf16[64,1024]{1,0:T(8,128)(2,1)S(1)} %fusion), channel_id=1, source_target_pairs={{0,64},{32,96},{64,0},{96,32},{1,65},{33,97},{65,1},{97,33},{2,66}... | collective-permute-start | bytes 393224 | tf_op jit(solution)/shard_map/ppermute | solution.py:345
  44.4 1.4 %shard_map.132 = (bf16[64,1024]{1,0:T(8,128)(2,1)S(1)}, bf16[128,2048]{1,0:T(8,128)(2,1)S(1)}, bf16[128,2048]{1,0:T(8,128)(2,1)S(1)}, bf16[128,2048]{1,0:T(8,128)(2,1)S(1)}) custom-call(bf16[2,64,1024]{2,1,0:T(8,128)(2,1)S(1)} %get-tuple-element.29.terms, bf16[128,2048]{1,0:T(8,128)(2,1)} %bitcast.11, bf16[128,2048]{1,0:T(8,128)(2,1)} %bitcast.13, ...), custom_call_target="tpu_custom_call" | custom-call | flops 1048576 | bytes 3145728 | tf_op jit(solution)/shard_map/pallas_call | solution.py:276
  45.8 6.1 %collective-permute-done.1.far = bf16[64,1024]{1,0:T(8,128)(2,1)S(1)} collective-permute-done((bf16[64,1024]{1,0:T(8,128)(2,1)S(1)}, bf16[64,1024]{1,0:T(8,128)(2,1)S(1)}, u32[]{:S(2)}, u32[]{:S(2)}) %collective-permute-start.1) | collective-permute-done | bytes 131104 | tf_op jit(solution)/shard_map/ppermute | solution.py:345
  51.9 0.0 all-to-all-done.1.data
  51.9 1.6 %shard_map.133 = (bf16[128,2048]{1,0:T(8,128)(2,1)}, bf16[128,2048]{1,0:T(8,128)(2,1)}, bf16[128,2048]{1,0:T(8,128)(2,1)}, f32[64,1024]{1,0:T(8,128)}) custom-call(bf16[32,128,128]{2,1,0:T(8,128)(2,1)S(1)} %all-to-all-done.1.data, bf16[2,64,1024]{2,1,0:T(8,128)(2,1)S(1)} %collective-permute-done.near, bf16[64,1024]{1,0:T(8,128)(2,1)S(1)} %collective-permute-done.1.far, ...), custom_call_target="tpu_custom_call" | custom-call | flops 1048576 | bytes 4194304 | tf_op jit(solution)/shard_map/pallas_call | solution.py:276
  (1 shorter events, 0.0 us)
Async XLA Ops:
  3.2 21.3 %all-to-all-start = ((bf16[32,128,128]{2,1,0:T(8,128)(2,1)}), bf16[32,128,128]{2,1,0:T(8,128)(2,1)S(1)}, u32[]{:S(2)}, u32[]{:S(2)}) async-start(bf16[32,128,128]{2,1,0:T(8,128)(2,1)} %shard_map.129), calls=%async_computation | async-start | bytes 2097152 | tf_op jit(solution)/shard_map/all_to_all | solution.py:290
  28.5 23.4 %all-to-all-start.1 = ((bf16[32,128,128]{2,1,0:T(8,128)(2,1)}), bf16[32,128,128]{2,1,0:T(8,128)(2,1)S(1)}, u32[]{:S(2)}, u32[]{:S(2)}) async-start(bf16[32,128,128]{2,1,0:T(8,128)(2,1)} %get-tuple-element.27), calls=%async_computation.1 | async-start | bytes 2097152 | tf_op jit(solution)/shard_map/all_to_all | solution.py:290
  32.5 9.1 %collective-permute-start = (bf16[2,64,1024]{2,1,0:T(8,128)(2,1)S(1)}, bf16[2,64,1024]{2,1,0:T(8,128)(2,1)S(1)}, u32[]{:S(2)}, u32[]{:S(2)}) collective-permute-start(bf16[2,64,1024]{2,1,0:T(8,128)(2,1)S(1)} %get-tuple-element.28), channel_id=1, source_target_pairs={{0,32},{32,0},{64,96},{96,64},{1,33},{33,1},{65,97},{97,65},{2,34}... | collective-permute-start | bytes 786440 | tf_op jit(solution)/shard_map/ppermute | solution.py:334
  41.7 10.2 %collective-permute-start.1 = (bf16[64,1024]{1,0:T(8,128)(2,1)S(1)}, bf16[64,1024]{1,0:T(8,128)(2,1)S(1)}, u32[]{:S(2)}, u32[]{:S(2)}) collective-permute-start(bf16[64,1024]{1,0:T(8,128)(2,1)S(1)} %fusion), channel_id=1, source_target_pairs={{0,64},{32,96},{64,0},{96,32},{1,65},{33,97},{65,1},{97,33},{2,66}... | collective-permute-start | bytes 393224 | tf_op jit(solution)/shard_map/ppermute | solution.py:345

commit v5 on v4

--- a/solution.py
+++ b/solution.py
@@ -21,7 +21,7 @@
 BF16 = jnp.bfloat16
 CHUNKS = 4
 GATE_BLOCKS = (10, 6)
-LATE_CHUNKS = 4
+LATE_BLOCKS = (6, 5, 5)
 STEPS = OWN // PAIR
 VMEM_LIMIT = 24 * 1024 * 1024
 
@@ -156,16 +156,15 @@
 
     @pl.when(core == 0)
     def _():
-        count = held.shape[2] // COLS // LATE_CHUNKS
-
-        @pl.loop(0, LATE_CHUNKS)
-        def _(chunk):
-            lanes = pl.ds(pl.multiple_of(chunk * count * COLS, COLS), count * COLS)
+        low = 0
+        for count in LATE_BLOCKS:
+            lanes = pl.ds(low * COLS, count * COLS)
             pairs = [(source.at[:, lanes], held.at[place, :, lanes]) for place, source in enumerate(sources)]
             wait_all(copies_of(pairs, in_sems))
-            gate_blocks(held, sent, chunk * count, count)
-            dests = pl.ds(2 * chunk * count, 2 * count)
+            gate_blocks(held, sent, low, count)
+            dests = pl.ds(2 * low, 2 * count)
             wait_all(copies_of([(sent.at[dests], out_hbm.at[dests])], out_sems))
+            low += count
 
 
 def filter_kernel(

time: 54.2 us -> 53.9 us (level)
  waiting for transfers between devices: 16.5 us -> 18.3 us
  starting transfers between devices: 24.4 us -> 22.6 us
    ppermute x1, starting transfers between devices: 7.98 us -> 5.76 us  [on_device(): near = lax.ppermute(sent_near, 'dp', [(d, d ^ 1) for d in range(4)])]
    ppermute x1, waiting for transfers between devices: 6.14 us -> 7.45 us  [on_device(): far = lax.ppermute(partial, 'dp', [(d, d ^ 2) for d in range(4)])]
    all_to_all x2, waiting for transfers between devices: 9.16 us -> 9.72 us  [swap(): return lax.all_to_all(array, 'seq', split_axis=0, concat_axis=0, tiled=True)]
where the time goes in v5:
time: 53.9 us; the launch traced here: 53.5 us
  starting transfers between devices  22.6 us (42%)
  waiting for transfers between devices  18.3 us (34%)
  Pallas kernels  11.9 us (22%)
  between operations  0.69 us (1%)
    all_to_all x2, starting transfers between devices, swap(): return lax.all_to_all(array, 'seq', split_axis=0, concat_axis=0, tiled=True)  14.1 us
    pallas_call x5, Pallas kernels, run(): pl.pallas_call(kernel, out_shape=tuple((spaces[p](x.shape, x.dtype) for x...  11.9 us
    all_to_all x2, waiting for transfers between devices, swap(): return lax.all_to_all(array, 'seq', split_axis=0, concat_axis=0, tiled=True)  9.72 us
    ppermute x1, waiting for transfers between devices, on_device(): far = lax.ppermute(partial, 'dp', [(d, d ^ 2) for d in range(4)])  7.45 us
    ppermute x1, starting transfers between devices, on_device(): near = lax.ppermute(sent_near, 'dp', [(d, d ^ 1) for d in range(4)])  5.76 us
    ppermute x1, starting transfers between devices, on_device(): far = lax.ppermute(partial, 'dp', [(d, d ^ 2) for d in range(4)])  2.7 us
    ppermute x1, waiting for transfers between devices, on_device(): near = lax.ppermute(sent_near, 'dp', [(d, d ^ 1) for d in range(4)])  1.16 us
  transfers between devices with their start and end apart: 4, of which 3 were waited for; matrix products, arithmetic and copies ran while one was open for 0% of the time, Pallas kernels for 7%

profile of v5, /device:TPU:1, one launch (start us, length us, event | category | flops | bytes accessed | tf_op | source)
XLA Modules:
  0.0 53.5 jit_solution(8980598925740255015)
XLA Ops:
  0.6 2.6 %shard_map.129 = bf16[32,128,128]{2,1,0:T(8,128)(2,1)} custom-call(s32[1]{0:T(128)} %bitcast.place_ref, bf16[128,2048]{1,0:T(8,128)(2,1)} %bitcast.16, bf16[128,2048]{1,0:T(8,128)(2,1)} %bitcast.10, bf16[128,2048]{1,0:T(8,128)(2,1)} %bitcast.12, bf16[128,2048]{1,0:T(8,128)(2,1)} %bitcast.14), custom_call_target="tpu_custom_call" | custom-call | flops 1048576 | bytes 3145728 | tf_op jit(solution)/shard_map/pallas_call | solution.py:275
  3.2 9.7 %all-to-all-start = ((bf16[32,128,128]{2,1,0:T(8,128)(2,1)}), bf16[32,128,128]{2,1,0:T(8,128)(2,1)S(1)}, u32[]{:S(2)}, u32[]{:S(2)}) async-start(bf16[32,128,128]{2,1,0:T(8,128)(2,1)} %shard_map.129), calls=%async_computation | async-start | bytes 2097152 | tf_op jit(solution)/shard_map/all_to_all | solution.py:289
  13.0 2.3 %shard_map.130 = (bf16[4,512,256]{2,1,0:T(8,128)(2,1)S(1)}, f32[2,32,128]{2,1,0:T(8,128)S(1)}, bf16[512,256]{1,0:T(8,128)(2,1)S(1)}, bf16[256,256]{1,0:T(8,128)(...) custom-call(f32[64,4096]{1,0:T(8,128)} %taps_hbm.1, f32[2,32,128]{2,1,0:T(8,128)} %constant.16.clone.twist_hbm, ...), custom_call_target="tpu_custom_call" | custom-call | flops 536870912 | bytes 3145728 | tf_op jit(solution)/shard_map/pallas_call | solution.py:275
  15.3 9.7 %all-to-all-done.data = bf16[32,128,128]{2,1,0:T(8,128)(2,1)S(1)} async-done(((bf16[32,128,128]{2,1,0:T(8,128)(2,1)}), bf16[32,128,128]{2,1,0:T(8,128)(2,1)S(1)}, u32[]{:S(2)}, u32[]{:S(2)}) %all-to-all-start) | async-done | bytes 1048608 | tf_op jit(solution)/shard_map/all_to_all | solution.py:289
  25.0 4.0 %shard_map.131 = (bf16[32,128,128]{2,1,0:T(8,128)(2,1)}, bf16[2,64,1024]{2,1,0:T(8,128)(2,1)S(1)}, bf16[2,64,1024]{2,1,0:T(8,128)(2,1)S(1)}) custom-call(s32[1]{0:T(128)} %bitcast.place_ref, bf16[32,128,128]{2,1,0:T(8,128)(2,1)S(1)} %all-to-all-done.data, bf16[4,512,256]{2,1,0:T(8,128)(2,1)S(1)} %get-tuple-element.21.filt, ...), custom_call_target="tpu_custom_call" | custom-call | flops 2147483648 | bytes 5242880 | tf_op jit(solution)/shard_map/pallas_call | solution.py:275
  29.0 4.4 %all-to-all-start.1 = ((bf16[32,128,128]{2,1,0:T(8,128)(2,1)}), bf16[32,128,128]{2,1,0:T(8,128)(2,1)S(1)}, u32[]{:S(2)}, u32[]{:S(2)}) async-start(bf16[32,128,128]{2,1,0:T(8,128)(2,1)} %get-tuple-element.27), calls=%async_computation.1 | async-start | bytes 2097152 | tf_op jit(solution)/shard_map/all_to_all | solution.py:289
  33.4 5.8 %collective-permute-start = (bf16[2,64,1024]{2,1,0:T(8,128)(2,1)S(1)}, bf16[2,64,1024]{2,1,0:T(8,128)(2,1)S(1)}, u32[]{:S(2)}, u32[]{:S(2)}) collective-permute-start(bf16[2,64,1024]{2,1,0:T(8,128)(2,1)S(1)} %get-tuple-element.28), channel_id=1, source_target_pairs={{0,32},{32,0},{64,96},{96,64},{1,33},{33,1},{65,97},{97,65},{2,34}... | collective-permute-start | bytes 786440 | tf_op jit(solution)/shard_map/ppermute | solution.py:333
  39.2 1.2 %collective-permute-done.near = bf16[2,64,1024]{2,1,0:T(8,128)(2,1)S(1)} collective-permute-done((bf16[2,64,1024]{2,1,0:T(8,128)(2,1)S(1)}, bf16[2,64,1024]{2,1,0:T(8,128)(2,1)S(1)}, u32[]{:S(2)}, u32[]{:S(2)}) %collective-permute-start) | collective-permute-done | bytes 262176 | tf_op jit(solution)/shard_map/ppermute | solution.py:333
  40.4 2.7 %collective-permute-start.1 = (bf16[64,1024]{1,0:T(8,128)(2,1)S(1)}, bf16[64,1024]{1,0:T(8,128)(2,1)S(1)}, u32[]{:S(2)}, u32[]{:S(2)}) collective-permute-start(bf16[64,1024]{1,0:T(8,128)(2,1)S(1)} %fusion), channel_id=1, source_target_pairs={{0,64},{32,96},{64,0},{96,32},{1,65},{33,97},{65,1},{97,33},{2,66}... | collective-permute-start | bytes 393224 | tf_op jit(solution)/shard_map/ppermute | solution.py:344
  43.1 1.4 %shard_map.132 = (bf16[64,1024]{1,0:T(8,128)(2,1)S(1)}, bf16[128,2048]{1,0:T(8,128)(2,1)S(1)}, bf16[128,2048]{1,0:T(8,128)(2,1)S(1)}, bf16[128,2048]{1,0:T(8,128)(2,1)S(1)}) custom-call(bf16[2,64,1024]{2,1,0:T(8,128)(2,1)S(1)} %get-tuple-element.29.terms, bf16[128,2048]{1,0:T(8,128)(2,1)} %bitcast.11, bf16[128,2048]{1,0:T(8,128)(2,1)} %bitcast.13, ...), custom_call_target="tpu_custom_call" | custom-call | flops 1048576 | bytes 3145728 | tf_op jit(solution)/shard_map/pallas_call | solution.py:275
  44.5 7.5 %collective-permute-done.1.far = bf16[64,1024]{1,0:T(8,128)(2,1)S(1)} collective-permute-done((bf16[64,1024]{1,0:T(8,128)(2,1)S(1)}, bf16[64,1024]{1,0:T(8,128)(2,1)S(1)}, u32[]{:S(2)}, u32[]{:S(2)}) %collective-permute-start.1) | collective-permute-done | bytes 131104 | tf_op jit(solution)/shard_map/ppermute | solution.py:344
  51.9 0.0 all-to-all-done.1.data
  51.9 1.6 %shard_map.133 = (bf16[128,2048]{1,0:T(8,128)(2,1)}, bf16[128,2048]{1,0:T(8,128)(2,1)}, bf16[128,2048]{1,0:T(8,128)(2,1)}, f32[64,1024]{1,0:T(8,128)}) custom-call(bf16[32,128,128]{2,1,0:T(8,128)(2,1)S(1)} %all-to-all-done.1.data, bf16[2,64,1024]{2,1,0:T(8,128)(2,1)S(1)} %collective-permute-done.near, bf16[64,1024]{1,0:T(8,128)(2,1)S(1)} %collective-permute-done.1.far, ...), custom_call_target="tpu_custom_call" | custom-call | flops 1048576 | bytes 4194304 | tf_op jit(solution)/shard_map/pallas_call | solution.py:275
  (1 shorter events, 0.0 us)
Async XLA Ops:
  3.2 21.8 %all-to-all-start = ((bf16[32,128,128]{2,1,0:T(8,128)(2,1)}), bf16[32,128,128]{2,1,0:T(8,128)(2,1)S(1)}, u32[]{:S(2)}, u32[]{:S(2)}) async-start(bf16[32,128,128]{2,1,0:T(8,128)(2,1)} %shard_map.129), calls=%async_computation | async-start | bytes 2097152 | tf_op jit(solution)/shard_map/all_to_all | solution.py:289
  29.0 22.9 %all-to-all-start.1 = ((bf16[32,128,128]{2,1,0:T(8,128)(2,1)}), bf16[32,128,128]{2,1,0:T(8,128)(2,1)S(1)}, u32[]{:S(2)}, u32[]{:S(2)}) async-start(bf16[32,128,128]{2,1,0:T(8,128)(2,1)} %get-tuple-element.27), calls=%async_computation.1 | async-start | bytes 2097152 | tf_op jit(solution)/shard_map/all_to_all | solution.py:289
  33.4 6.9 %collective-permute-start = (bf16[2,64,1024]{2,1,0:T(8,128)(2,1)S(1)}, bf16[2,64,1024]{2,1,0:T(8,128)(2,1)S(1)}, u32[]{:S(2)}, u32[]{:S(2)}) collective-permute-start(bf16[2,64,1024]{2,1,0:T(8,128)(2,1)S(1)} %get-tuple-element.28), channel_id=1, source_target_pairs={{0,32},{32,0},{64,96},{96,64},{1,33},{33,1},{65,97},{97,65},{2,34}... | collective-permute-start | bytes 786440 | tf_op jit(solution)/shard_map/ppermute | solution.py:333
  40.4 11.5 %collective-permute-start.1 = (bf16[64,1024]{1,0:T(8,128)(2,1)S(1)}, bf16[64,1024]{1,0:T(8,128)(2,1)S(1)}, u32[]{:S(2)}, u32[]{:S(2)}) collective-permute-start(bf16[64,1024]{1,0:T(8,128)(2,1)S(1)} %fusion), channel_id=1, source_target_pairs={{0,64},{32,96},{64,0},{96,32},{1,65},{33,97},{65,1},{97,33},{2,66}... | collective-permute-start | bytes 393224 | tf_op jit(solution)/shard_map/ppermute | solution.py:344

commit v6 on v5

--- a/solution.py
+++ b/solution.py
@@ -201,14 +201,14 @@
 def conv_kernel(place_ref, data, filt, twist, first, ahead, last, back, out_hbm, own, near, out, terms, out_sems):
     leaving = []
     prods, cross = [], []
-    for many in range(0, STEPS, 2):
+    for many in range(0, STEPS, 4):
         blocks = []
-        for step in range(many, many + 2):
+        for step in range(many, many + 4):
             for part in range(2):
                 rows = slice(part * OWN + step * PAIR, part * OWN + (step + 1) * PAIR)
                 blocks.append(split_rows(data[:, rows, :]))
         specs = spectra(blocks, twist, first, ahead)
-        for step in range(many, many + 2):
+        for step in range(many, many + 4):
             low = (step - many) * 4 * BLOCK
             gated, grads, turn = specs[low : low + 2 * BLOCK], specs[low + 2 * BLOCK : low + 4 * BLOCK], filt[step]
             cross.append(product(gated, grads, True).astype(BF16))

time: 53.9 us -> 53.8 us (level)
  no operation moved by 1% of the time
where the time goes in v6:
time: 53.8 us; the launch traced here: 53.4 us
  starting transfers between devices  22.6 us (42%)
  waiting for transfers between devices  18.3 us (34%)
  Pallas kernels  11.8 us (22%)
  between operations  0.69 us (1%)
    all_to_all x2, starting transfers between devices, swap(): return lax.all_to_all(array, 'seq', split_axis=0, concat_axis=0, tiled=True)  14.1 us
    pallas_call x5, Pallas kernels, run(): pl.pallas_call(kernel, out_shape=tuple((spaces[p](x.shape, x.dtype) for x...  11.8 us
    all_to_all x2, waiting for transfers between devices, swap(): return lax.all_to_all(array, 'seq', split_axis=0, concat_axis=0, tiled=True)  9.72 us
    ppermute x1, waiting for transfers between devices, on_device(): far = lax.ppermute(partial, 'dp', [(d, d ^ 2) for d in range(4)])  7.45 us
    ppermute x1, starting transfers between devices, on_device(): near = lax.ppermute(sent_near, 'dp', [(d, d ^ 1) for d in range(4)])  5.76 us
    ppermute x1, starting transfers between devices, on_device(): far = lax.ppermute(partial, 'dp', [(d, d ^ 2) for d in range(4)])  2.7 us
    ppermute x1, waiting for transfers between devices, on_device(): near = lax.ppermute(sent_near, 'dp', [(d, d ^ 1) for d in range(4)])  1.16 us
  transfers between devices with their start and end apart: 4, of which 3 were waited for; matrix products, arithmetic and copies ran while one was open for 0% of the time, Pallas kernels for 7%

profile of v6, /device:TPU:1, one launch (start us, length us, event | category | flops | bytes accessed | tf_op | source)
XLA Modules:
  0.0 53.4 jit_solution(11780600094394110729)
XLA Ops:
  0.6 2.6 %shard_map.129 = bf16[32,128,128]{2,1,0:T(8,128)(2,1)} custom-call(s32[1]{0:T(128)} %bitcast.place_ref, bf16[128,2048]{1,0:T(8,128)(2,1)} %bitcast.16, bf16[128,2048]{1,0:T(8,128)(2,1)} %bitcast.10, bf16[128,2048]{1,0:T(8,128)(2,1)} %bitcast.12, bf16[128,2048]{1,0:T(8,128)(2,1)} %bitcast.14), custom_call_target="tpu_custom_call" | custom-call | flops 1048576 | bytes 3145728 | tf_op jit(solution)/shard_map/pallas_call | solution.py:275
  3.2 9.7 %all-to-all-start = ((bf16[32,128,128]{2,1,0:T(8,128)(2,1)}), bf16[32,128,128]{2,1,0:T(8,128)(2,1)S(1)}, u32[]{:S(2)}, u32[]{:S(2)}) async-start(bf16[32,128,128]{2,1,0:T(8,128)(2,1)} %shard_map.129), calls=%async_computation | async-start | bytes 2097152 | tf_op jit(solution)/shard_map/all_to_all | solution.py:289
  13.0 2.3 %shard_map.130 = (bf16[4,512,256]{2,1,0:T(8,128)(2,1)S(1)}, f32[2,32,128]{2,1,0:T(8,128)S(1)}, bf16[512,256]{1,0:T(8,128)(2,1)S(1)}, bf16[256,256]{1,0:T(8,128)(...) custom-call(f32[64,4096]{1,0:T(8,128)} %taps_hbm.1, f32[2,32,128]{2,1,0:T(8,128)} %constant.16.clone.twist_hbm, ...), custom_call_target="tpu_custom_call" | custom-call | flops 536870912 | bytes 3145728 | tf_op jit(solution)/shard_map/pallas_call | solution.py:275
  15.3 9.7 %all-to-all-done.data = bf16[32,128,128]{2,1,0:T(8,128)(2,1)S(1)} async-done(((bf16[32,128,128]{2,1,0:T(8,128)(2,1)}), bf16[32,128,128]{2,1,0:T(8,128)(2,1)S(1)}, u32[]{:S(2)}, u32[]{:S(2)}) %all-to-all-start) | async-done | bytes 1048608 | tf_op jit(solution)/shard_map/all_to_all | solution.py:289
  25.0 3.9 %shard_map.131 = (bf16[32,128,128]{2,1,0:T(8,128)(2,1)}, bf16[2,64,1024]{2,1,0:T(8,128)(2,1)S(1)}, bf16[2,64,1024]{2,1,0:T(8,128)(2,1)S(1)}) custom-call(s32[1]{0:T(128)} %bitcast.place_ref, bf16[32,128,128]{2,1,0:T(8,128)(2,1)S(1)} %all-to-all-done.data, bf16[4,512,256]{2,1,0:T(8,128)(2,1)S(1)} %get-tuple-element.21.filt, ...), custom_call_target="tpu_custom_call" | custom-call | flops 2147483648 | bytes 5242880 | tf_op jit(solution)/shard_map/pallas_call | solution.py:275
  28.9 4.4 %all-to-all-start.1 = ((bf16[32,128,128]{2,1,0:T(8,128)(2,1)}), bf16[32,128,128]{2,1,0:T(8,128)(2,1)S(1)}, u32[]{:S(2)}, u32[]{:S(2)}) async-start(bf16[32,128,128]{2,1,0:T(8,128)(2,1)} %get-tuple-element.27), calls=%async_computation.1 | async-start | bytes 2097152 | tf_op jit(solution)/shard_map/all_to_all | solution.py:289
  33.3 5.8 %collective-permute-start = (bf16[2,64,1024]{2,1,0:T(8,128)(2,1)S(1)}, bf16[2,64,1024]{2,1,0:T(8,128)(2,1)S(1)}, u32[]{:S(2)}, u32[]{:S(2)}) collective-permute-start(bf16[2,64,1024]{2,1,0:T(8,128)(2,1)S(1)} %get-tuple-element.28), channel_id=1, source_target_pairs={{0,32},{32,0},{64,96},{96,64},{1,33},{33,1},{65,97},{97,65},{2,34}... | collective-permute-start | bytes 786440 | tf_op jit(solution)/shard_map/ppermute | solution.py:333
  39.0 1.2 %collective-permute-done.near = bf16[2,64,1024]{2,1,0:T(8,128)(2,1)S(1)} collective-permute-done((bf16[2,64,1024]{2,1,0:T(8,128)(2,1)S(1)}, bf16[2,64,1024]{2,1,0:T(8,128)(2,1)S(1)}, u32[]{:S(2)}, u32[]{:S(2)}) %collective-permute-start) | collective-permute-done | bytes 262176 | tf_op jit(solution)/shard_map/ppermute | solution.py:333
  40.2 2.7 %collective-permute-start.1 = (bf16[64,1024]{1,0:T(8,128)(2,1)S(1)}, bf16[64,1024]{1,0:T(8,128)(2,1)S(1)}, u32[]{:S(2)}, u32[]{:S(2)}) collective-permute-start(bf16[64,1024]{1,0:T(8,128)(2,1)S(1)} %fusion), channel_id=1, source_target_pairs={{0,64},{32,96},{64,0},{96,32},{1,65},{33,97},{65,1},{97,33},{2,66}... | collective-permute-start | bytes 393224 | tf_op jit(solution)/shard_map/ppermute | solution.py:344
  42.9 1.4 %shard_map.132 = (bf16[64,1024]{1,0:T(8,128)(2,1)S(1)}, bf16[128,2048]{1,0:T(8,128)(2,1)S(1)}, bf16[128,2048]{1,0:T(8,128)(2,1)S(1)}, bf16[128,2048]{1,0:T(8,128)(2,1)S(1)}) custom-call(bf16[2,64,1024]{2,1,0:T(8,128)(2,1)S(1)} %get-tuple-element.29.terms, bf16[128,2048]{1,0:T(8,128)(2,1)} %bitcast.11, bf16[128,2048]{1,0:T(8,128)(2,1)} %bitcast.13, ...), custom_call_target="tpu_custom_call" | custom-call | flops 1048576 | bytes 3145728 | tf_op jit(solution)/shard_map/pallas_call | solution.py:275
  44.3 7.5 %collective-permute-done.1.far = bf16[64,1024]{1,0:T(8,128)(2,1)S(1)} collective-permute-done((bf16[64,1024]{1,0:T(8,128)(2,1)S(1)}, bf16[64,1024]{1,0:T(8,128)(2,1)S(1)}, u32[]{:S(2)}, u32[]{:S(2)}) %collective-permute-start.1) | collective-permute-done | bytes 131104 | tf_op jit(solution)/shard_map/ppermute | solution.py:344
  51.8 0.0 all-to-all-done.1.data
  51.8 1.6 %shard_map.133 = (bf16[128,2048]{1,0:T(8,128)(2,1)}, bf16[128,2048]{1,0:T(8,128)(2,1)}, bf16[128,2048]{1,0:T(8,128)(2,1)}, f32[64,1024]{1,0:T(8,128)}) custom-call(bf16[32,128,128]{2,1,0:T(8,128)(2,1)S(1)} %all-to-all-done.1.data, bf16[2,64,1024]{2,1,0:T(8,128)(2,1)S(1)} %collective-permute-done.near, bf16[64,1024]{1,0:T(8,128)(2,1)S(1)} %collective-permute-done.1.far, ...), custom_call_target="tpu_custom_call" | custom-call | flops 1048576 | bytes 4194304 | tf_op jit(solution)/shard_map/pallas_call | solution.py:275
  (1 shorter events, 0.0 us)
Async XLA Ops:
  3.2 21.8 %all-to-all-start = ((bf16[32,128,128]{2,1,0:T(8,128)(2,1)}), bf16[32,128,128]{2,1,0:T(8,128)(2,1)S(1)}, u32[]{:S(2)}, u32[]{:S(2)}) async-start(bf16[32,128,128]{2,1,0:T(8,128)(2,1)} %shard_map.129), calls=%async_computation | async-start | bytes 2097152 | tf_op jit(solution)/shard_map/all_to_all | solution.py:289
  28.9 22.9 %all-to-all-start.1 = ((bf16[32,128,128]{2,1,0:T(8,128)(2,1)}), bf16[32,128,128]{2,1,0:T(8,128)(2,1)S(1)}, u32[]{:S(2)}, u32[]{:S(2)}) async-start(bf16[32,128,128]{2,1,0:T(8,128)(2,1)} %get-tuple-element.27), calls=%async_computation.1 | async-start | bytes 2097152 | tf_op jit(solution)/shard_map/all_to_all | solution.py:289
  33.3 6.9 %collective-permute-start = (bf16[2,64,1024]{2,1,0:T(8,128)(2,1)S(1)}, bf16[2,64,1024]{2,1,0:T(8,128)(2,1)S(1)}, u32[]{:S(2)}, u32[]{:S(2)}) collective-permute-start(bf16[2,64,1024]{2,1,0:T(8,128)(2,1)S(1)} %get-tuple-element.28), channel_id=1, source_target_pairs={{0,32},{32,0},{64,96},{96,64},{1,33},{33,1},{65,97},{97,65},{2,34}... | collective-permute-start | bytes 786440 | tf_op jit(solution)/shard_map/ppermute | solution.py:333
  40.2 11.5 %collective-permute-start.1 = (bf16[64,1024]{1,0:T(8,128)(2,1)S(1)}, bf16[64,1024]{1,0:T(8,128)(2,1)S(1)}, u32[]{:S(2)}, u32[]{:S(2)}) collective-permute-start(bf16[64,1024]{1,0:T(8,128)(2,1)S(1)} %fusion), channel_id=1, source_target_pairs={{0,64},{32,96},{64,0},{96,32},{1,65},{33,97},{65,1},{97,33},{2,66}... | collective-permute-start | bytes 393224 | tf_op jit(solution)/shard_map/ppermute | solution.py:344
